TPU v7x, 128 devices: a whole 4x4x4 slice. The times are simulated.
128 devices in a mesh: row: 16 (over x, y), col: 8 (over z, core).
Axes of the slice: x: 4, y: 4, z: 4, core: 2. Of those that a mesh axis runs over, the one named last changes fastest.
Arguments:
- eigvec: float32 [196608, 512], P(None, ('row', 'col')), may hold values from -6 to 6
- house: float32 [8, 196608, 256], P(None, ('row', 'col')), may hold values from -0.02734375 to 0.02734375
- tri: float32 [8, 256, 256], replicated, may hold values from -1 to 1.5, as said below
Outputs:
- back_vectors: float32 [196608, 512], P(('row', 'col'))
Inputs may be any that keep to these rules, and one draw needn't show every extreme that they name: `tri`: each block upper triangular; diagonal between 0.5 and 1.5.
All inputs are finite; a program needn't handle non-finite values.
Results may differ from a plain program's by a relative error of at most 0.00012.
Values sent between devices are 32-bit elements; how exact they have to be, the bound alone decides.
No kernel may reach another device: no remote copies, remote signals or barrier semaphores. Data moves between devices by JAX's collectives and lax.ppermute only.
A program may use at most 192 MiB of HBM per device.

v0:
```python
import jax
import jax.numpy as jnp
from jax import lax
from jax.sharding import PartitionSpec as P


def matmul(left, right):
    return jnp.dot(left, right, precision=lax.Precision.HIGHEST, preferred_element_type=jnp.float32)


def inner(left, right):
    return lax.dot_general(
        left,
        right,
        (((0,), (0,)), ((), ())),
        precision=lax.Precision.HIGHEST,
        preferred_element_type=jnp.float32,
    )


def local(eigvec, house, tri):
    local_rows = lax.all_to_all(eigvec, ("row", "col"), split_axis=0, concat_axis=1, tiled=True)
    blocks = house.shape[0]
    middle = local_rows
    for number in range(blocks):
        proj = lax.psum(inner(house[number], middle), ("row", "col"))
        middle = middle - matmul(house[number], matmul(tri[number], proj))
    return middle


def solution(mesh):
    in_specs = (P(None, ("row", "col")), P(None, ("row", "col"), None), P())
    out_specs = P(("row", "col"), None)
    return jax.shard_map(local, mesh=mesh, in_specs=in_specs, out_specs=out_specs, check_vma=False)
```

profile of v0, /device:TPU:1, one launch (start us, length us, event | category | flops | bytes accessed | tf_op | source)
XLA Modules:
  0.0 1322.2 jit_solution(14749609707894769475)
XLA Ops:
  6.5 53.4 %all_to_all.19 = f32[128,1536,4]{1,2,0:T(4,128)} all-to-all(f32[128,1536,4]{1,2,0:T(4,128)} %bitcast.153), channel_id=1, replica_groups=mesh['row'=16,'col'=8] {'row','col'}, dimensions={0} | all-to-all | bytes 6291456 | tf_op jit(solution)/shard_map/all_to_all | solution.py:22
  60.0 3.2 all_to_all.17
  63.2 7.4 fusion.30
  71.2 140.7 %all-reduce.9.cloned.1.call-done = f32[256,512]{1,0:T(8,128)} async-done(((f32[256,512]{1,0:T(8,128)}), f32[256,512]{1,0:T(8,128)}) %all-reduce.9.cloned.1.call-update) | async-done | bytes 524304 | tf_op jit(solution)/shard_map/psum | solution.py:26
  211.8 2.1 fusion.83
  214.0 4.4 fusion.7
  220.1 4.8 fusion.48
  225.2 143.8 %all-reduce.11.cloned.1.call-done = f32[256,512]{0,1:T(8,128)} async-done(((f32[256,512]{0,1:T(8,128)}), f32[256,512]{0,1:T(8,128)}) %all-reduce.11.cloned.1.call-update) | async-done | bytes 524304 | tf_op jit(solution)/shard_map/psum | solution.py:26
  370.7 5.1 fusion.6
  375.8 4.8 fusion.51
  380.9 143.7 %all-reduce.13.cloned.1.call-done = f32[256,512]{0,1:T(8,128)} async-done(((f32[256,512]{0,1:T(8,128)}), f32[256,512]{0,1:T(8,128)}) %all-reduce.13.cloned.1.call-update) | async-done | bytes 524304 | tf_op jit(solution)/shard_map/psum | solution.py:26
  524.6 1.7 fusion.79
  526.3 4.4 fusion.5
  532.4 4.8 fusion.54
  537.6 143.7 %all-reduce.15.cloned.1.call-done = f32[256,512]{0,1:T(8,128)} async-done(((f32[256,512]{0,1:T(8,128)}), f32[256,512]{0,1:T(8,128)}) %all-reduce.15.cloned.1.call-update) | async-done | bytes 524304 | tf_op jit(solution)/shard_map/psum | solution.py:26
  681.3 1.7 fusion.77
  683.0 5.1 fusion.4
  688.1 4.8 fusion.57
  693.3 143.6 %all-reduce.17.cloned.1.call-done = f32[256,512]{0,1:T(8,128)} async-done(((f32[256,512]{0,1:T(8,128)}), f32[256,512]{0,1:T(8,128)}) %all-reduce.17.cloned.1.call-update) | async-done | bytes 524304 | tf_op jit(solution)/shard_map/psum | solution.py:26
  838.7 4.4 fusion.3
  844.8 4.8 fusion.60
  850.2 143.4 %all-reduce.19.cloned.1.call-done = f32[256,512]{0,1:T(8,128)} async-done(((f32[256,512]{0,1:T(8,128)}), f32[256,512]{0,1:T(8,128)}) %all-reduce.19.cloned.1.call-update) | async-done | bytes 524304 | tf_op jit(solution)/shard_map/psum | solution.py:26
  993.6 1.7 fusion.73
  995.4 5.1 fusion.2
  1000.5 4.8 fusion.63
  1005.6 143.7 %all-reduce.21.cloned.1.call-done = f32[256,512]{0,1:T(8,128)} async-done(((f32[256,512]{0,1:T(8,128)}), f32[256,512]{0,1:T(8,128)}) %all-reduce.21.cloned.1.call-update) | async-done | bytes 524304 | tf_op jit(solution)/shard_map/psum | solution.py:26
  1151.0 4.4 fusion.1
  1157.1 4.8 fusion.66
  1162.0 144.0 %all-reduce.23.cloned.1.call-done = f32[256,512]{0,1:T(8,128)} async-done(((f32[256,512]{0,1:T(8,128)}), f32[256,512]{0,1:T(8,128)}) %all-reduce.23.cloned.1.call-update) | async-done | bytes 524304 | tf_op jit(solution)/shard_map/psum | solution.py:26
  1306.0 1.7 fusion.69
  1307.7 5.1 fusion
  1312.8 2.4 copy.5
  (27 shorter events, 14.4 us)
Async XLA Ops:
  6.5 205.3 %all-reduce.9.cloned.1.call-start = ((), (), s32[]{:S(2)}) async-start(), calls=%async_computation.1 | async-start | bytes 1048576 | tf_op jit(solution)/shard_map/psum | solution.py:26
  70.6 298.4 %all-reduce.11.cloned.1.call-start = ((), (), s32[]{:S(2)}) async-start(), calls=%async_computation.2 | async-start | bytes 1048576 | tf_op jit(solution)/shard_map/psum | solution.py:26
  218.4 1.7 copy-start
  224.9 299.7 %all-reduce.13.cloned.1.call-start = ((), (), s32[]{:S(2)}) async-start(), calls=%async_computation.3 | async-start | bytes 1048576 | tf_op jit(solution)/shard_map/psum | solution.py:26
  380.6 300.6 %all-reduce.15.cloned.1.call-start = ((), (), s32[]{:S(2)}) async-start(), calls=%async_computation.4 | async-start | bytes 1048576 | tf_op jit(solution)/shard_map/psum | solution.py:26
  530.8 1.7 copy-start.1
  537.3 299.6 %all-reduce.17.cloned.1.call-start = ((), (), s32[]{:S(2)}) async-start(), calls=%async_computation.5 | async-start | bytes 1048576 | tf_op jit(solution)/shard_map/psum | solution.py:26
  693.0 300.7 %all-reduce.19.cloned.1.call-start = ((), (), s32[]{:S(2)}) async-start(), calls=%async_computation.6 | async-start | bytes 1048576 | tf_op jit(solution)/shard_map/psum | solution.py:26
  843.1 1.7 copy-start.2
  849.6 299.6 %all-reduce.21.cloned.1.call-start = ((), (), s32[]{:S(2)}) async-start(), calls=%async_computation.7 | async-start | bytes 1048576 | tf_op jit(solution)/shard_map/psum | solution.py:26
  1005.3 300.6 %all-reduce.23.cloned.1.call-start = ((), (), s32[]{:S(2)}) async-start(), calls=%async_computation.8 | async-start | bytes 1048576 | tf_op jit(solution)/shard_map/psum | solution.py:26
  1155.5 1.7 copy-start.3
Sparse Core Ops, SparseCore 0:
  70.7 141.0 all-reduce.8
  225.1 143.8 all-reduce.10
  380.8 143.7 all-reduce.12
  537.4 143.8 all-reduce.14
  693.1 143.7 all-reduce.16
  849.8 143.8 all-reduce.18
  1005.5 143.7 all-reduce.20
  1162.1 143.8 all-reduce.22
where the time goes:
time: 1330 us; the launch traced here: 1320 us
  waiting for transfers between devices  1150 us (86%)
  matrix products  93.6 us (7%)
  blocking collectives  53.4 us (4%)
  between operations  13.9 us (1%)
    psum x8, waiting for transfers between devices, local(): proj = lax.psum(inner(house[number], middle), ('row', 'col'))  1150 us
    all_to_all x1, blocking collectives, local(): lax.all_to_all(eigvec, ('row', 'col'), split_axis=0, concat_axis=1, tiled...  53.4 us
    dot_general x16, matrix products, matmul(): jnp.dot(left, right, precision=lax.Precision.HIGHEST, preferred_element_t...  52.3 us
    dot_general x8, matrix products, inner(): lax.dot_general(left, right, (((0,), (0,)), ((), ())), precision=lax.Prec...  41.2 us
  transfers between devices with their start and end apart: 8, of which 8 were waited for; matrix products, arithmetic and copies ran while one was open for 0% of the time, Pallas kernels for 0%

commit v1 on v0

v1 whole, which is shorter than its diff:
```python
import jax
import jax.numpy as jnp
from jax import lax
from jax.experimental import pallas as pl
from jax.experimental.pallas import tpu as pltpu
from jax.sharding import PartitionSpec as P

BF = jnp.bfloat16
F32 = jnp.float32
AXES = ("row", "col")
NN = ((1,), (0,))
NT = ((1,), (1,))
LIMIT = 56 * 1024 * 1024


def split(x):
    high = x.astype(BF)
    return high, (x - high.astype(F32)).astype(BF)


def dot(a, b, dims=NN):
    return lax.dot_general(a, b, (dims, ((), ())), preferred_element_type=F32)


def dot3(ah, al, bh, bl):
    return dot(ah, bh) + (dot(ah, bl) + dot(al, bh))


def gram_kernel(core_ref, h_ref, keep_ref, send_ref, th, tl, xh, xl):
    b = pl.program_id(0)
    core = core_ref[0]
    width = h_ref.shape[2]
    half_pairs = keep_ref.shape[0] // (2 * width)
    x = h_ref[0]
    high, low = split(x)
    xh[...] = high
    xl[...] = low

    @pl.when(b < pl.num_programs(0) - 1)
    def _():
        t_high, t_low = split(x.T)
        at = pl.ds(pl.multiple_of(b * width, width), width)
        th[at, :] = t_high
        tl[at, :] = t_low

    def pair(a, carry):
        at = pl.ds(pl.multiple_of(a * width, width), width)
        g = dot3(th[at, :], tl[at, :], xh[...], xl[...])
        p = b * (b - 1) // 2 + a
        half = (p >= half_pairs).astype(jnp.int32)
        q = p - half_pairs * half
        first = pl.ds(pl.multiple_of(q * 2 * width, width), width)
        second = pl.ds(pl.multiple_of(q * 2 * width + width, width), width)

        @pl.when(half == core)
        def _():
            keep_ref[first, :] = g[:, :128]
            keep_ref[second, :] = g[:, 128:]

        @pl.when(half != core)
        def _():
            send_ref[first, :] = g[:, :128]
            send_ref[second, :] = g[:, 128:]

        return carry

    lax.fori_loop(0, b, pair, 0)


def gram_call(core, house):
    blocks, rows, width = house.shape
    pairs = blocks * (blocks - 1) // 2
    out = jax.ShapeDtypeStruct((pairs // 2 * 2 * width, 128), F32)
    whole = pl.BlockSpec(out.shape, lambda b, c: (0, 0))
    return pl.pallas_call(
        gram_kernel,
        grid_spec=pltpu.PrefetchScalarGridSpec(
            num_scalar_prefetch=1,
            grid=(blocks,),
            in_specs=[pl.BlockSpec((1, rows, width), lambda b, c: (b, 0, 0))],
            out_specs=[whole, whole],
            scratch_shapes=[
                pltpu.VMEM(((blocks - 1) * width, rows), BF),
                pltpu.VMEM(((blocks - 1) * width, rows), BF),
                pltpu.VMEM((rows, width), BF),
                pltpu.VMEM((rows, width), BF),
            ],
        ),
        out_shape=[out, out],
        compiler_params=pltpu.CompilerParams(vmem_limit_bytes=LIMIT),
        cost_estimate=pl.CostEstimate(flops=6 * pairs * rows * width * width, bytes_accessed=20_000_000, transcendentals=0),
        name="gram",
    )(core, house)


def unpack(x_ref, t):
    at = t * 128 if isinstance(t, int) else pl.multiple_of(t * 128, 128)
    return x_ref[:, :, pl.ds(at, 128)].reshape(-1, 128)


def proj_kernel(half_ref, x_ref, h_ref, out_ref, eh, el):
    b = pl.program_id(0)
    steps = h_ref.shape[1] // 128
    groups = out_ref.shape[0] // eh.shape[0]

    @pl.when(b == 0)
    def _():
        for t in range(steps):
            high, low = split(unpack(x_ref, t))
            eh[:, t * 128:(t + 1) * 128] = high
            el[:, t * 128:(t + 1) * 128] = low

    high, low = split(h_ref[0])
    p = dot3(eh[...], el[...], high, low)
    n = p.shape[0]
    out_ref[pl.ds(2 * b, n, stride=groups), :] = p[:, :128]
    out_ref[pl.ds(2 * b + 1, n, stride=groups), :] = p[:, 128:]


def proj_call(half, x, house):
    blocks, rows, width = house.shape
    sources, cols = x.shape[0] // 2, x.shape[1]
    n = sources * cols
    groups = blocks * width // 128
    return pl.pallas_call(
        proj_kernel,
        grid_spec=pltpu.PrefetchScalarGridSpec(
            num_scalar_prefetch=1,
            grid=(blocks,),
            in_specs=[
                pl.BlockSpec((sources, cols, rows), lambda b, h: (h[0], 0, 0)),
                pl.BlockSpec((1, rows, width), lambda b, h: (b, 0, 0)),
            ],
            out_specs=pl.BlockSpec((n * groups, 128), lambda b, h: (0, 0)),
            scratch_shapes=[
                pltpu.VMEM((n, rows), BF),
                pltpu.VMEM((n, rows), BF),
            ],
        ),
        out_shape=jax.ShapeDtypeStruct((n * groups, 128), F32),
        compiler_params=pltpu.CompilerParams(vmem_limit_bytes=LIMIT),
        cost_estimate=pl.CostEstimate(flops=6 * blocks * n * rows * width, bytes_accessed=16_000_000, transcendentals=0),
        name="proj",
    )(half, x, house)


def stacked(x):
    high = x.astype(BF).astype(F32)
    return jnp.concatenate([high, x - high], axis=0).astype(BF)


def times(x, right, dims):
    n = x.shape[0]
    high, low = split(right)
    s = stacked(x)
    r = dot(s, high, dims) + dot(s, low, dims)
    return r[:n] + r[n:]


def solve_kernel(core_ref, p_ref, mine_ref, other_ref, tri_ref, out_ref):
    blocks, width = tri_ref.shape[0], tri_ref.shape[1]
    groups = 2 * blocks
    n = p_ref.shape[0] // groups
    half_pairs = blocks * (blocks - 1) // 4

    def run(halves):
        coefs = []
        for b in range(blocks):
            p = jnp.concatenate([p_ref[pl.ds(2 * b, n, stride=groups), :], p_ref[pl.ds(2 * b + 1, n, stride=groups), :]], axis=1)
            for a in range(b):
                pair = b * (b - 1) // 2 + a
                ref = halves[pair // half_pairs]
                at = pair % half_pairs * 2 * width
                g = jnp.concatenate([ref[at:at + width, :], ref[at + width:at + 2 * width, :]], axis=1)
                p = p - times(coefs[a], g, NN)
            coef = times(p, tri_ref[b], NT)
            coefs.append(coef)
            out_ref[pl.ds(2 * b, n, stride=groups), :] = coef[:, :128]
            out_ref[pl.ds(2 * b + 1, n, stride=groups), :] = coef[:, 128:]

    @pl.when(core_ref[0] == 0)
    def _():
        run((mine_ref, other_ref))

    @pl.when(core_ref[0] != 0)
    def _():
        run((other_ref, mine_ref))


def solve_call(core, p, mine, other, tri):
    vmem = pl.BlockSpec(memory_space=pltpu.VMEM)
    return pl.pallas_call(
        solve_kernel,
        in_specs=[pl.BlockSpec(memory_space=pltpu.SMEM), vmem, vmem, vmem, vmem],
        out_specs=vmem,
        out_shape=jax.ShapeDtypeStruct(p.shape, F32),
        compiler_params=pltpu.CompilerParams(vmem_limit_bytes=LIMIT),
        cost_estimate=pl.CostEstimate(flops=8_000_000_000, bytes_accessed=10_000_000, transcendentals=0),
        name="solve",
    )(core, p, mine, other, tri)


def update_kernel(half_ref, c_ref, x_ref, h_ref, *rest):
    out_ref, ch, cl = rest[-3:]
    r = pl.program_id(0)
    blocks, tile, width = h_ref.shape
    groups = blocks * width // 128
    n = c_ref.shape[0] // groups
    here = tile // 128

    @pl.when(r == 0)
    def _():
        for g in range(groups):
            high, low = split(c_ref[pl.ds(g, n, stride=groups), :].T)
            ch[g * 128:(g + 1) * 128, :] = high
            cl[g * 128:(g + 1) * 128, :] = low

    total = jnp.zeros((tile, n), F32)
    for b in range(blocks):
        high, low = split(h_ref[b])
        at = slice(b * width, (b + 1) * width)
        total = total + dot3(high, low, ch[at, :], cl[at, :])
    for t in range(here):
        e = unpack(x_ref, r * here + t)
        out_ref[t * 128:(t + 1) * 128, :] = e.T - total[t * 128:(t + 1) * 128, :]


def update_call(half, coef, x, house, prev, tile=512):
    blocks, rows, width = house.shape
    sources, cols = x.shape[0] // 2, x.shape[1]
    n = sources * cols
    whole = lambda r, h: (0, 0)
    in_specs = [
        pl.BlockSpec(coef.shape, whole),
        pl.BlockSpec((sources, cols, rows), lambda r, h: (h[0], 0, 0)),
        pl.BlockSpec((blocks, tile, width), lambda r, h: (0, r, 0)),
    ]
    args = [half, coef, x, house]
    aliases = {}
    if prev is not None:
        in_specs.append(pl.BlockSpec(memory_space=pl.ANY))
        args.append(prev)
        aliases = {4: 0}
    return pl.pallas_call(
        update_kernel,
        grid_spec=pltpu.PrefetchScalarGridSpec(
            num_scalar_prefetch=1,
            grid=(rows // tile,),
            in_specs=in_specs,
            out_specs=pl.BlockSpec((tile, n), lambda r, h: (r, h[0])),
            scratch_shapes=[
                pltpu.VMEM((blocks * width, n), BF),
                pltpu.VMEM((blocks * width, n), BF),
            ],
        ),
        out_shape=jax.ShapeDtypeStruct((rows, 2 * n), F32),
        input_output_aliases=aliases,
        compiler_params=pltpu.CompilerParams(vmem_limit_bytes=LIMIT),
        cost_estimate=pl.CostEstimate(flops=6 * blocks * n * rows * width, bytes_accessed=18_000_000, transcendentals=0),
        name="update",
    )(*args)


def pair_swap(x):
    return lax.ppermute(x, "col", [(i, i ^ 1) for i in range(lax.axis_size("col"))])


def all_to_all(x):
    return lax.all_to_all(x, AXES, 0, 0, tiled=True)


def scatter_sum(x, devices):
    got = all_to_all(x).reshape(devices // 2, 2, x.shape[0] // devices, 128)
    return jnp.sum(got, axis=0)


def spread(x, devices):
    sent = jnp.broadcast_to(x[None], (devices // 2,) + x.shape)
    return all_to_all(sent.reshape(-1, 128))


def local(eigvec, house, tri):
    blocks, rows, width = house.shape
    cols = eigvec.shape[1]
    devices = eigvec.shape[0] // rows
    core = lax.rem(lax.axis_index("col"), 2).astype(jnp.int32).reshape(1)
    away = 1 - core

    with jax.named_scope("rows"):
        sent = eigvec.reshape(devices, rows, cols).transpose(0, 2, 1)
        x = all_to_all(sent)
    with jax.named_scope("gram"):
        keep, send = gram_call(core, house)
        share = scatter_sum(keep + pair_swap(send), devices)
        mine = spread(share, devices)
        other = pair_swap(mine)
    with jax.named_scope("proj"):
        send = pair_swap(proj_call(away, x, house))
        proj = scatter_sum(proj_call(core, x, house) + send, devices)
    with jax.named_scope("solve"):
        coef = solve_call(core, proj.reshape(-1, 128), mine, other, tri)
    with jax.named_scope("gather"):
        near = spread(coef.reshape(2, -1, 128), devices)
        far = pair_swap(near)
    with jax.named_scope("update"):
        out = update_call(core, near, x, house, None)
        out = update_call(away, far, x, house, out)
    return out


def solution(mesh):
    in_specs = (P(None, AXES), P(None, AXES, None), P())
    out_specs = P(AXES, None)
    return jax.shard_map(local, mesh=mesh, in_specs=in_specs, out_specs=out_specs, check_vma=False)
```

time: 1330 us -> 321 us (0.24)
  waiting for transfers between devices: 1150 us -> 79.6 us
  matrix products: 93.6 us -> 0 us
  Pallas kernels: 0 us -> 86.5 us
  blocking collectives: 53.4 us -> 126 us
  between operations: 13.9 us -> 0.05 us
    psum x8 -> x0, waiting for transfers between devices: 1150 us -> none  [local(): proj = lax.psum(inner(house[number], middle), ('row', 'col'))]
    dot_general x24 -> x0, matrix products: 93.6 us -> none  [the longest x16 52.3 us: matmul(): jnp.dot(left, right, precision=lax.Precision.HIGHEST, preferred_element_t...]
    pallas_call x0 -> x6, Pallas kernels: none -> 86.5 us  [the longest x1 32.3 us: gram_call(): pl.pallas_call(gram_kernel, grid_spec=pltpu.PrefetchScalarGridSpec(num_sc...]
    all_to_all x0 -> x2, waiting for transfers between devices: none -> 73.3 us  [all_to_all(): return lax.all_to_all(x, AXES, 0, 0, tiled=True)]
    all_to_all x1 -> x3, blocking collectives: 53.4 us -> 126 us  [all_to_all(): return lax.all_to_all(x, AXES, 0, 0, tiled=True)]
  transfers between devices with their start and end apart: 8 -> 6, of which waited for: 8 -> 3; matrix products, arithmetic and copies ran while one was open for 0% -> 1% of each run, Pallas kernels for 0% -> 11%
where the time goes in v1:
time: 321 us; the launch traced here: 320 us
  blocking collectives  126 us (39%)
  Pallas kernels  86.5 us (27%)
  waiting for transfers between devices  79.6 us (25%)
  starting transfers between devices  15 us (5%)
  other arithmetic  7.2 us (2%)
  local copies, waits for them, and re-layouts  5.43 us (2%)
    all_to_all x3, blocking collectives, all_to_all(): return lax.all_to_all(x, AXES, 0, 0, tiled=True)  126 us
    all_to_all x2, waiting for transfers between devices, all_to_all(): return lax.all_to_all(x, AXES, 0, 0, tiled=True)  73.3 us
    pallas_call x1, Pallas kernels, gram_call(): pl.pallas_call(gram_kernel, grid_spec=pltpu.PrefetchScalarGridSpec(num_sc...  32.3 us
    pallas_call x2, Pallas kernels, proj_call(): pl.pallas_call(proj_kernel, grid_spec=pltpu.PrefetchScalarGridSpec(num_sc...  25 us
    pallas_call x2, Pallas kernels, update_call(): pl.pallas_call(update_kernel, grid_spec=pltpu.PrefetchScalarGridSpec(num_...  22.2 us
    all_to_all x2, starting transfers between devices, all_to_all(): return lax.all_to_all(x, AXES, 0, 0, tiled=True)  10.1 us
    pallas_call x1, Pallas kernels, solve_call(): pl.pallas_call(solve_kernel, in_specs=[pl.BlockSpec(memory_space=pltpu.SM...  7.04 us
  transfers between devices with their start and end apart: 6, of which 3 were waited for; matrix products, arithmetic and copies ran while one was open for 1% of the time, Pallas kernels for 11%

profile of v1, /device:TPU:1, one launch (start us, length us, event | category | flops | bytes accessed | tf_op | source)
XLA Modules:
  0.0 320.2 jit_solution(13217846232970149568)
XLA Ops:
  0.0 32.3 %gram.1 = (f32[7168,128]{1,0:T(8,128)}, f32[7168,128]{1,0:T(8,128)}) custom-call(s32[1]{0:T(128)} %bitcast.half_ref.core_ref, f32[8,1536,256]{2,1,0:T(8,128)} %h_ref.9), custom_call_target="tpu_custom_call" | custom-call | flops 16911433728 | bytes 20000000 | tf_op jit(solution)/shard_map/gram/gram/pallas_call | solution.py:75
  32.3 1.4 collective-permute-start.1
  33.7 6.2 %collective-permute-done.1 = f32[7168,128]{1,0:T(8,128)S(1)} collective-permute-done((f32[7168,128]{1,0:T(8,128)}, f32[7168,128]{1,0:T(8,128)S(1)}, u32[]{:S(2)}, u32[]{:S(2)}) %collective-permute-start.1) | collective-permute-done | bytes 3670048 | tf_op jit(solution)/shard_map/gram/ppermute | solution.py:265
  40.0 2.4 add.7
  42.4 57.9 %all_to_all.45 = f32[128,56,128]{2,1,0:T(8,128)} all-to-all(f32[128,56,128]{2,1,0:T(8,128)S(1)} %bitcast.16), channel_id=1, replica_groups=mesh['row'=16,'col'=8] {'row','col'}, dimensions={0} | all-to-all | bytes 7340032 | tf_op jit(solution)/shard_map/gram/all_to_all | solution.py:269
  100.3 4.5 %all-to-all-start = ((f32[128,4,1536]{2,1,0:T(4,128)}), f32[128,4,1536]{2,1,0:T(4,128)S(1)}, u32[]{:S(2)}, u32[]{:S(2)}) async-start(f32[128,4,1536]{2,1,0:T(4,128)} %bitcast.22), calls=%async_computation | async-start | bytes 6291456 | tf_op jit(solution)/shard_map/rows/all_to_all | solution.py:269
  104.8 2.2 reduce_sum.19
  107.0 39.7 %all-to-all-done.x_ref = f32[128,4,1536]{2,1,0:T(4,128)S(1)} async-done(((f32[128,4,1536]{2,1,0:T(4,128)}), f32[128,4,1536]{2,1,0:T(4,128)S(1)}, u32[]{:S(2)}, u32[]{:S(2)}) %all-to-all-start) | async-done | bytes 3145760 | tf_op jit(solution)/shard_map/rows/all_to_all | solution.py:269
  146.8 0.0 copy-start
  146.8 2.2 broadcast_in_dim.6
  149.0 0.7 copy-done
  149.6 5.6 %all-to-all-start.3 = ((f32[128,56,128]{2,1,0:T(8,128)}), f32[128,56,128]{2,1,0:T(8,128)}, u32[]{:S(2)}, u32[]{:S(2)}) async-start(f32[128,56,128]{2,1,0:T(8,128)} %bitcast.14), calls=%async_computation.3 | async-start | bytes 7340032 | tf_op jit(solution)/shard_map/gram/all_to_all | solution.py:269
  155.2 12.5 %proj.3 = f32[4096,128]{1,0:T(8,128)} custom-call(s32[1]{0:T(128)S(6)} %sub.3.half_ref, f32[128,4,1536]{2,1,0:T(4,128)} %copy-done, f32[8,1536,256]{2,1,0:T(8,128)} %h_ref.9), custom_call_target="tpu_custom_call" | custom-call | flops 4831838208 | bytes 16000000 | tf_op jit(solution)/shard_map/proj/proj/pallas_call | solution.py:125
  167.7 1.3 collective-permute-start
  169.0 33.6 %all-to-all-done.3 = f32[128,56,128]{2,1,0:T(8,128)} async-done(((f32[128,56,128]{2,1,0:T(8,128)}), f32[128,56,128]{2,1,0:T(8,128)}, u32[]{:S(2)}, u32[]{:S(2)}) %all-to-all-start.3) | async-done | bytes 3670048 | tf_op jit(solution)/shard_map/gram/all_to_all | solution.py:269
  202.6 1.0 collective-permute-start.2
  203.6 12.5 %proj.2 = f32[4096,128]{1,0:T(8,128)} custom-call(s32[1]{0:T(128)} %bitcast.half_ref.core_ref, f32[128,4,1536]{2,1,0:T(4,128)} %copy-done, f32[8,1536,256]{2,1,0:T(8,128)} %h_ref.9), custom_call_target="tpu_custom_call" | custom-call | flops 4831838208 | bytes 16000000 | tf_op jit(solution)/shard_map/proj/proj/pallas_call | solution.py:125
  216.1 0.0 collective-permute-done
  216.1 1.8 add.6
  217.9 33.9 %all_to_all.46 = f32[128,32,128]{2,1,0:T(8,128)S(1)} all-to-all(f32[128,32,128]{2,1,0:T(8,128)S(1)} %bitcast.19), channel_id=1, replica_groups=mesh['row'=16,'col'=8] {'row','col'}, dimensions={0} | all-to-all | bytes 4194304 | tf_op jit(solution)/shard_map/proj/all_to_all | solution.py:269
  251.8 0.8 reduce_sum.18
  252.6 0.0 collective-permute-done.2.other_ref
  252.6 7.0 %solve.1 = f32[64,128]{1,0:T(8,128)} custom-call(s32[1]{0:T(128)} %bitcast.half_ref.core_ref, f32[64,128]{1,0:T(8,128)} %bitcast.23, f32[7168,128]{1,0:T(8,128)} %bitcast.9.mine_ref, f32[7168,128]{1,0:T(8,128)} %collective-permute-done.2.other_ref, f32[8,256,256]{2,1,0:T(8,128)} %tri_ref.1), custom_call_target="tpu_custom_call" | custom-call | flops 8000000000 | bytes 10000000 | tf_op jit(solution)/shard_map/solve/solve/pallas_call | solution.py:192
  259.6 1.0 broadcast_in_dim.15
  260.6 34.7 %all_to_all.47 = f32[128,32,128]{2,1,0:T(8,128)S(1)} all-to-all(f32[128,32,128]{2,1,0:T(8,128)S(1)} %bitcast.21), channel_id=1, replica_groups=mesh['row'=16,'col'=8] {'row','col'}, dimensions={0} | all-to-all | bytes 4194304 | tf_op jit(solution)/shard_map/gather/all_to_all | solution.py:269
  295.3 0.0 copy-start.1
  295.3 1.2 collective-permute-start.3
  296.4 0.2 copy-done.1
  296.6 11.1 %update.2.rest_0_ = f32[1536,512]{1,0:T(8,128)} custom-call(s32[1]{0:T(128)} %bitcast.half_ref.core_ref, f32[4096,128]{1,0:T(8,128)} %bitcast.18, f32[128,4,1536]{2,1,0:T(4,128)} %copy-done, f32[8,1536,256]{2,1,0:T(8,128)} %h_ref.9), custom_call_target="tpu_custom_call" | custom-call | flops 4831838208 | bytes 18000000 | tf_op jit(solution)/shard_map/update/update/pallas_call | solution.py:244
  307.7 0.0 collective-permute-done.3.c_ref
  307.7 1.4 copy-done.2
  309.1 11.1 %update.3 = f32[1536,512]{1,0:T(8,128)} custom-call(s32[1]{0:T(128)S(6)} %sub.3.half_ref, f32[4096,128]{1,0:T(8,128)} %copy-done.2, f32[128,4,1536]{2,1,0:T(4,128)} %copy-done, f32[8,1536,256]{2,1,0:T(8,128)} %h_ref.9, f32[1536,512]{1,0:T(8,128)} %update.2.rest_0_), custom_call_target="tpu_custom_call", output_to_operand_aliasing={{}: (4, {})} | custom-call | flops 4831838208 | bytes 18000000 | tf_op jit(solution)/shard_map/update/update/pallas_call | solution.py:244
  (1 shorter events, 0.0 us)
Async XLA Ops:
  32.3 7.7 %collective-permute-start.1 = (f32[7168,128]{1,0:T(8,128)}, f32[7168,128]{1,0:T(8,128)S(1)}, u32[]{:S(2)}, u32[]{:S(2)}) collective-permute-start(f32[7168,128]{1,0:T(8,128)} %get-tuple-element.8), channel_id=1, source_target_pairs={{0,1},{1,0},{2,3},{3,2},{4,5},{5,4},{6,7},{7,6},{8,9},{9,8},{10,11... | collective-permute-start | bytes 11010056 | tf_op jit(solution)/shard_map/gram/ppermute | solution.py:265
  100.3 46.5 %all-to-all-start = ((f32[128,4,1536]{2,1,0:T(4,128)}), f32[128,4,1536]{2,1,0:T(4,128)S(1)}, u32[]{:S(2)}, u32[]{:S(2)}) async-start(f32[128,4,1536]{2,1,0:T(4,128)} %bitcast.22), calls=%async_computation | async-start | bytes 6291456 | tf_op jit(solution)/shard_map/rows/all_to_all | solution.py:269
  146.8 2.9 copy-start
  149.6 52.9 %all-to-all-start.3 = ((f32[128,56,128]{2,1,0:T(8,128)}), f32[128,56,128]{2,1,0:T(8,128)}, u32[]{:S(2)}, u32[]{:S(2)}) async-start(f32[128,56,128]{2,1,0:T(8,128)} %bitcast.14), calls=%async_computation.3 | async-start | bytes 7340032 | tf_op jit(solution)/shard_map/gram/all_to_all | solution.py:269
  167.7 48.4 %collective-permute-start = (f32[4096,128]{1,0:T(8,128)}, f32[4096,128]{1,0:T(8,128)S(1)}, u32[]{:S(2)}, u32[]{:S(2)}) collective-permute-start(f32[4096,128]{1,0:T(8,128)} %proj.3), channel_id=1, source_target_pairs={{0,1},{1,0},{2,3},{3,2},{4,5},{5,4},{6,7},{7,6},{8,9},{9,8},{10,11... | collective-permute-start | bytes 6291464 | tf_op jit(solution)/shard_map/proj/ppermute | solution.py:265
  202.6 50.0 %collective-permute-start.2 = (f32[7168,128]{1,0:T(8,128)}, f32[7168,128]{1,0:T(8,128)}, u32[]{:S(2)}, u32[]{:S(2)}) collective-permute-start(f32[7168,128]{1,0:T(8,128)} %bitcast.9.mine_ref), channel_id=1, source_target_pairs={{0,1},{1,0},{2,3},{3,2},{4,5},{5,4},{6,7},{7,6},{8,9},{9,8},{10,11... | collective-permute-start | bytes 11010056 | tf_op jit(solution)/shard_map/gram/ppermute | solution.py:265
  295.3 1.4 copy-start.1
  295.3 12.4 %collective-permute-start.3 = (f32[4096,128]{1,0:T(8,128)S(1)}, f32[4096,128]{1,0:T(8,128)S(1)}, u32[]{:S(2)}, u32[]{:S(2)}) collective-permute-start(f32[4096,128]{1,0:T(8,128)S(1)} %bitcast.17), channel_id=1, source_target_pairs={{0,1},{1,0},{2,3},{3,2},{4,5},{5,4},{6,7},{7,6},{8,9},{9,8},{10,11... | collective-permute-start | bytes 6291464 | tf_op jit(solution)/shard_map/gather/ppermute | solution.py:265
  307.7 1.4 copy-start.2

commit v2 on v1

--- a/solution.py
+++ b/solution.py
@@ -1,3 +1,5 @@
+import functools
+
 import jax
 import jax.numpy as jnp
 from jax import lax
@@ -28,13 +30,30 @@
 
 def gram_kernel(core_ref, h_ref, keep_ref, send_ref, th, tl, xh, xl):
     b = pl.program_id(0)
-    core = core_ref[0]
+    first_core = core_ref[0] == 0
     width = h_ref.shape[2]
-    half_pairs = keep_ref.shape[0] // (2 * width)
+    chunks = width // 8
+    runs = keep_ref.shape[0] // chunks
     x = h_ref[0]
     high, low = split(x)
     xh[...] = high
     xl[...] = low
+
+    def strip(top):
+        for a in range(0, top, 2):
+            count = min(2, top - a)
+            at = slice(a * width, (a + count) * width)
+            g = dot3(th[at, :], tl[at, :], xh[...], xl[...])
+            for i in range(count):
+                p = top * (top - 1) // 2 + a + i
+                left = g[i * width:(i + 1) * width, :128].reshape(chunks, 8, 128)
+                right = g[i * width:(i + 1) * width, 128:].reshape(chunks, 8, 128)
+                to = pl.ds(p % runs * chunks, chunks)
+                keep_ref[to, p // runs] = jnp.where(first_core, left, right)
+                send_ref[to, p // runs] = jnp.where(first_core, right, left)
+
+    for top in range(1, th.shape[0] // width + 1):
+        pl.when(b == top)(functools.partial(strip, top))
 
     @pl.when(b < pl.num_programs(0) - 1)
     def _():
@@ -43,35 +62,12 @@
         th[at, :] = t_high
         tl[at, :] = t_low
 
-    def pair(a, carry):
-        at = pl.ds(pl.multiple_of(a * width, width), width)
-        g = dot3(th[at, :], tl[at, :], xh[...], xl[...])
-        p = b * (b - 1) // 2 + a
-        half = (p >= half_pairs).astype(jnp.int32)
-        q = p - half_pairs * half
-        first = pl.ds(pl.multiple_of(q * 2 * width, width), width)
-        second = pl.ds(pl.multiple_of(q * 2 * width + width, width), width)
-
-        @pl.when(half == core)
-        def _():
-            keep_ref[first, :] = g[:, :128]
-            keep_ref[second, :] = g[:, 128:]
-
-        @pl.when(half != core)
-        def _():
-            send_ref[first, :] = g[:, :128]
-            send_ref[second, :] = g[:, 128:]
-
-        return carry
-
-    lax.fori_loop(0, b, pair, 0)
-
-
-def gram_call(core, house):
+
+def gram_call(core, house, pieces):
     blocks, rows, width = house.shape
     pairs = blocks * (blocks - 1) // 2
-    out = jax.ShapeDtypeStruct((pairs // 2 * 2 * width, 128), F32)
-    whole = pl.BlockSpec(out.shape, lambda b, c: (0, 0))
+    out = jax.ShapeDtypeStruct((pieces, pairs * width // 8 // pieces, 8, 128), F32)
+    whole = pl.BlockSpec(out.shape, lambda b, c: (0, 0, 0, 0))
     return pl.pallas_call(
         gram_kernel,
         grid_spec=pltpu.PrefetchScalarGridSpec(
@@ -88,7 +84,7 @@
         ),
         out_shape=[out, out],
         compiler_params=pltpu.CompilerParams(vmem_limit_bytes=LIMIT),
-        cost_estimate=pl.CostEstimate(flops=6 * pairs * rows * width * width, bytes_accessed=20_000_000, transcendentals=0),
+        cost_estimate=pl.CostEstimate(flops=12 * pairs * rows * width * width, bytes_accessed=20_000_000, transcendentals=0),
         name="gram",
     )(core, house)
 
@@ -144,60 +140,47 @@
     )(half, x, house)
 
 
-def stacked(x):
-    high = x.astype(BF).astype(F32)
-    return jnp.concatenate([high, x - high], axis=0).astype(BF)
-
-
-def times(x, right, dims):
-    n = x.shape[0]
-    high, low = split(right)
-    s = stacked(x)
-    r = dot(s, high, dims) + dot(s, low, dims)
-    return r[:n] + r[n:]
-
-
-def solve_kernel(core_ref, p_ref, mine_ref, other_ref, tri_ref, out_ref):
+def solve_kernel(p_ref, g_ref, tri_ref, out_ref, ch, cl):
     blocks, width = tri_ref.shape[0], tri_ref.shape[1]
     groups = 2 * blocks
     n = p_ref.shape[0] // groups
-    half_pairs = blocks * (blocks - 1) // 4
-
-    def run(halves):
-        coefs = []
-        for b in range(blocks):
-            p = jnp.concatenate([p_ref[pl.ds(2 * b, n, stride=groups), :], p_ref[pl.ds(2 * b + 1, n, stride=groups), :]], axis=1)
-            for a in range(b):
-                pair = b * (b - 1) // 2 + a
-                ref = halves[pair // half_pairs]
-                at = pair % half_pairs * 2 * width
-                g = jnp.concatenate([ref[at:at + width, :], ref[at + width:at + 2 * width, :]], axis=1)
-                p = p - times(coefs[a], g, NN)
-            coef = times(p, tri_ref[b], NT)
-            coefs.append(coef)
-            out_ref[pl.ds(2 * b, n, stride=groups), :] = coef[:, :128]
-            out_ref[pl.ds(2 * b + 1, n, stride=groups), :] = coef[:, 128:]
-
-    @pl.when(core_ref[0] == 0)
-    def _():
-        run((mine_ref, other_ref))
-
-    @pl.when(core_ref[0] != 0)
-    def _():
-        run((other_ref, mine_ref))
-
-
-def solve_call(core, p, mine, other, tri):
+    chunks = width // 8
+    runs = g_ref.shape[0] // chunks
+    deep = g_ref.shape[1] // 2
+    for b in range(blocks):
+        p = jnp.concatenate([p_ref[pl.ds(2 * b, n, stride=groups), :], p_ref[pl.ds(2 * b + 1, n, stride=groups), :]], axis=1)
+        for a in range(b):
+            pair = b * (b - 1) // 2 + a
+            at = pl.ds(pair % runs * chunks, chunks)
+            g = [g_ref[at, half * deep + pair // runs].reshape(width, 128) for half in range(2)]
+            high, low = split(jnp.concatenate(g, axis=1))
+            own = slice(a * width, (a + 1) * width)
+            p = p - dot3(ch[:, own], cl[:, own], high, low)
+        high, low = split(p)
+        t_high, t_low = split(tri_ref[b])
+        coef = dot(high, t_high, NT) + (dot(high, t_low, NT) + dot(low, t_high, NT))
+        high, low = split(coef)
+        own = slice(b * width, (b + 1) * width)
+        ch[:, own] = high
+        cl[:, own] = low
+        out_ref[pl.ds(2 * b, n, stride=groups), :] = coef[:, :128]
+        out_ref[pl.ds(2 * b + 1, n, stride=groups), :] = coef[:, 128:]
+
+
+def solve_call(p, gram, tri):
+    blocks, width = tri.shape[0], tri.shape[1]
+    n = p.shape[0] // (2 * blocks)
     vmem = pl.BlockSpec(memory_space=pltpu.VMEM)
     return pl.pallas_call(
         solve_kernel,
-        in_specs=[pl.BlockSpec(memory_space=pltpu.SMEM), vmem, vmem, vmem, vmem],
+        in_specs=[vmem, vmem, vmem],
         out_specs=vmem,
         out_shape=jax.ShapeDtypeStruct(p.shape, F32),
+        scratch_shapes=[pltpu.VMEM((n, blocks * width), BF), pltpu.VMEM((n, blocks * width), BF)],
         compiler_params=pltpu.CompilerParams(vmem_limit_bytes=LIMIT),
-        cost_estimate=pl.CostEstimate(flops=8_000_000_000, bytes_accessed=10_000_000, transcendentals=0),
+        cost_estimate=pl.CostEstimate(flops=4_000_000_000, bytes_accessed=13_000_000, transcendentals=0),
         name="solve",
-    )(core, p, mine, other, tri)
+    )(p, gram, tri)
 
 
 def update_kernel(half_ref, c_ref, x_ref, h_ref, *rest):
@@ -269,14 +252,16 @@
     return lax.all_to_all(x, AXES, 0, 0, tiled=True)
 
 
-def scatter_sum(x, devices):
-    got = all_to_all(x).reshape(devices // 2, 2, x.shape[0] // devices, 128)
-    return jnp.sum(got, axis=0)
-
-
-def spread(x, devices):
-    sent = jnp.broadcast_to(x[None], (devices // 2,) + x.shape)
-    return all_to_all(sent.reshape(-1, 128))
+def sums(got, devices):
+    return jnp.sum(got.reshape(devices // 2, 2, -1, 128), axis=0)
+
+
+def copies(x, devices):
+    return jnp.broadcast_to(x[None], (devices // 2,) + x.shape).reshape(-1, 128)
+
+
+def after(x, *others):
+    return lax.optimization_barrier((x,) + others)[0]
 
 
 def local(eigvec, house, tri):
@@ -287,20 +272,29 @@
     away = 1 - core
 
     with jax.named_scope("rows"):
-        sent = eigvec.reshape(devices, rows, cols).transpose(0, 2, 1)
-        x = all_to_all(sent)
+        x = all_to_all(eigvec.reshape(devices, rows, cols).transpose(0, 2, 1))
+    always = core[0] >= 0
     with jax.named_scope("gram"):
-        keep, send = gram_call(core, house)
-        share = scatter_sum(keep + pair_swap(send), devices)
-        mine = spread(share, devices)
-        other = pair_swap(mine)
+        keep, send = (part.reshape(-1, 128) for part in gram_call(core, house, devices))
+        keep = lax.cond(always, lambda keep, send: keep + pair_swap(send), lambda keep, send: keep, keep, send)
+        got = all_to_all(after(keep, x))
     with jax.named_scope("proj"):
         send = pair_swap(proj_call(away, x, house))
-        proj = scatter_sum(proj_call(core, x, house) + send, devices)
+        proj = proj_call(core, x, house) + send
+    with jax.named_scope("gram"):
+        got, proj = lax.optimization_barrier((got, proj))
+        share = sums(got, devices)
+        gram = lax.all_gather(share.reshape(-1, 128), AXES, axis=0, tiled=True)
+        gram = gram.reshape(devices, -1, 8, 128)
+
+    def exchange(proj):
+        with jax.named_scope("proj"):
+            proj = sums(all_to_all(proj), devices)
+            return all_to_all(copies(proj, devices))
+
+    proj = lax.cond(always, exchange, lambda proj: proj, after(proj, share))
     with jax.named_scope("solve"):
-        coef = solve_call(core, proj.reshape(-1, 128), mine, other, tri)
-    with jax.named_scope("gather"):
-        near = spread(coef.reshape(2, -1, 128), devices)
+        near = solve_call(proj, gram, tri)
         far = pair_swap(near)
     with jax.named_scope("update"):
         out = update_call(core, near, x, house, None)

time: 321 us -> 262 us (0.82)
  blocking collectives: 126 us -> 73.2 us
  waiting for transfers between devices: 79.6 us -> 52.2 us
  between operations: 0.05 us -> 13.4 us
  starting transfers between devices: 15 us -> 21.7 us
  other arithmetic: 7.2 us -> 10.6 us
    all_to_all x3 -> x2, blocking collectives: 126 us -> 73.2 us  [all_to_all(): return lax.all_to_all(x, AXES, 0, 0, tiled=True)]
    all_to_all x2, waiting for transfers between devices: 73.3 us -> 21 us  [all_to_all(): return lax.all_to_all(x, AXES, 0, 0, tiled=True)]
    all_gather x0 -> x1, waiting for transfers between devices: none -> 25 us  [local(): gram = lax.all_gather(share.reshape(-1, 128), AXES, axis=0, tiled=True)]
    all_to_all x2, starting transfers between devices: 10.1 us -> 19.2 us  [all_to_all(): return lax.all_to_all(x, AXES, 0, 0, tiled=True)]
    pallas_call x1, Pallas kernels: 32.3 us -> 28.5 us  [gram_call(): pl.pallas_call(gram_kernel, grid_spec=pltpu.PrefetchScalarGridSpec(num_sc...]
    pallas_call x1, Pallas kernels: 7.04 us -> 10.8 us  [solve_call(): pl.pallas_call(solve_kernel, in_specs=[vmem, vmem, vmem], out_specs=vmem,...]
  transfers between devices with their start and end apart: 6 -> 6, of which waited for: 3 -> 4; matrix products, arithmetic and copies ran while one was open for 1% -> 3% of each run, Pallas kernels for 11% -> 25%
where the time goes in v2:
time: 262 us; the launch traced here: 261 us
  Pallas kernels  86.5 us (33%)
  blocking collectives  73.2 us (28%)
  waiting for transfers between devices  52.2 us (20%)
  starting transfers between devices  21.7 us (8%)
  between operations  13.4 us (5%)
  other arithmetic  10.6 us (4%)
  local copies, waits for them, and re-layouts  3.29 us (1%)
    all_to_all x2, blocking collectives, all_to_all(): return lax.all_to_all(x, AXES, 0, 0, tiled=True)  73.2 us
    pallas_call x1, Pallas kernels, gram_call(): pl.pallas_call(gram_kernel, grid_spec=pltpu.PrefetchScalarGridSpec(num_sc...  28.5 us
    all_gather x1, waiting for transfers between devices, local(): gram = lax.all_gather(share.reshape(-1, 128), AXES, axis=0, tiled=True)  25 us
    pallas_call x2, Pallas kernels, proj_call(): pl.pallas_call(proj_kernel, grid_spec=pltpu.PrefetchScalarGridSpec(num_sc...  25 us
    pallas_call x2, Pallas kernels, update_call(): pl.pallas_call(update_kernel, grid_spec=pltpu.PrefetchScalarGridSpec(num_...  22.2 us
    all_to_all x2, waiting for transfers between devices, all_to_all(): return lax.all_to_all(x, AXES, 0, 0, tiled=True)  21 us
    all_to_all x2, starting transfers between devices, all_to_all(): return lax.all_to_all(x, AXES, 0, 0, tiled=True)  19.2 us
    pallas_call x1, Pallas kernels, solve_call(): pl.pallas_call(solve_kernel, in_specs=[vmem, vmem, vmem], out_specs=vmem,...  10.8 us
  transfers between devices with their start and end apart: 6, of which 4 were waited for; matrix products, arithmetic and copies ran while one was open for 3% of the time, Pallas kernels for 25%

profile of v2, /device:TPU:1, one launch (start us, length us, event | category | flops | bytes accessed | tf_op | source)
XLA Modules:
  0.0 261.0 jit_solution(8917998391791245290)
XLA Ops:
  6.5 11.5 %all-to-all-start.2 = ((f32[128,4,1536]{2,1,0:T(4,128)}), f32[128,4,1536]{2,1,0:T(4,128)S(1)}, u32[]{:S(2)}, u32[]{:S(2)}) async-start(f32[128,4,1536]{2,1,0:T(4,128)} %bitcast.22), calls=%async_computation.2 | async-start | bytes 6291456 | tf_op jit(solution)/shard_map/rows/all_to_all | solution.py:252
  18.0 28.5 %gram.1 = (f32[128,7,8,128]{3,2,1,0:T(8,128)}, f32[128,7,8,128]{3,2,1,0:T(8,128)}) custom-call(s32[1]{0:T(128)} %bitcast.5.core_ref.half_ref, f32[8,1536,256]{2,1,0:T(8,128)} %h_ref.9), custom_call_target="tpu_custom_call" | custom-call | flops 33822867456 | bytes 20000000 | tf_op jit(solution)/shard_map/gram/gram/pallas_call | solution.py:71
  46.6 11.5 %conditional.2 = (f32[7168,128]{1,0:T(8,128)}) conditional(s32[]{:T(128)} %convert_element_type.4, f32[7168,128]{1,0:T(8,128)} %bitcast.15, (f32[128,7,8,128]{3,2,1,0:T(8,128)}, f32[7168,128]{1,0:T(8,128)}) %tuple.30), branch_computations={%region_0.0_spmd, %region_1.0_spmd} | conditional | flops 917504 | bytes 25690160 | solution.py:279
  46.6 1.1 collective-permute-start
  47.7 6.2 %collective-permute-done = f32[7168,128]{1,0:T(8,128)S(1)} collective-permute-done((f32[7168,128]{1,0:T(8,128)}, f32[7168,128]{1,0:T(8,128)S(1)}, u32[]{:S(2)}, u32[]{:S(2)}) %collective-permute-start) | collective-permute-done | bytes 3670048 | tf_op jit(solution)/shard_map/gram/cond/branch_1_fun/ppermute | solution.py:248
  53.9 4.2 %add.4 = f32[7168,128]{1,0:T(8,128)} add(f32[7168,128]{1,0:T(8,128)} %get-tuple-element.19, f32[7168,128]{1,0:T(8,128)S(1)} %collective-permute-done) | non-fusion elementwise | flops 917504 | bytes 11010048 | tf_op jit(solution)/shard_map/gram/cond/branch_1_fun/add | solution.py:279
  58.1 1.7 all-to-all-done.2.x_ref
  59.9 0.0 copy-start
  59.9 1.7 copy-done
  61.6 7.7 %all-to-all-start.3 = ((f32[128,56,128]{2,1,0:T(8,128)}), f32[128,56,128]{2,1,0:T(8,128)}, u32[]{:S(2)}, u32[]{:S(2)}) async-start(f32[128,56,128]{2,1,0:T(8,128)} %bitcast.17), calls=%async_computation.3 | async-start | bytes 7340032 | tf_op jit(solution)/shard_map/gram/all_to_all | solution.py:252
  69.3 0.0 all-gather.2.cloned.1.call-start
  69.4 12.5 %proj.3 = f32[4096,128]{1,0:T(8,128)} custom-call(s32[1]{0:T(128)S(6)} %sub.3.half_ref, f32[128,4,1536]{2,1,0:T(4,128)} %copy-done, f32[8,1536,256]{2,1,0:T(8,128)} %h_ref.9), custom_call_target="tpu_custom_call" | custom-call | flops 4831838208 | bytes 16000000 | tf_op jit(solution)/shard_map/proj/proj/pallas_call | solution.py:121
  81.9 1.1 collective-permute-start.1
  83.0 12.5 %proj.2 = f32[4096,128]{1,0:T(8,128)} custom-call(s32[1]{0:T(128)} %bitcast.5.core_ref.half_ref, f32[128,4,1536]{2,1,0:T(4,128)} %copy-done, f32[8,1536,256]{2,1,0:T(8,128)} %h_ref.9), custom_call_target="tpu_custom_call" | custom-call | flops 4831838208 | bytes 16000000 | tf_op jit(solution)/shard_map/proj/proj/pallas_call | solution.py:121
  95.5 0.0 collective-permute-done.1
  95.5 1.8 add.6
  97.3 19.2 %all-to-all-done.3 = f32[128,56,128]{2,1,0:T(8,128)} async-done(((f32[128,56,128]{2,1,0:T(8,128)}), f32[128,56,128]{2,1,0:T(8,128)}, u32[]{:S(2)}, u32[]{:S(2)}) %all-to-all-start.3) | async-done | bytes 3670048 | tf_op jit(solution)/shard_map/gram/all_to_all | solution.py:252
  116.5 2.9 %reduce_sum.18 = f32[2,56,128]{2,1,0:T(8,128)} reduce(f32[64,2,56,128]{3,2,1,0:T(8,128)} %bitcast.11, f32[]{:T(128)} %constant.15.clone.1), dimensions={0}, to_apply=%region_2.0 | reduce | flops 903168 | bytes 3727364 | tf_op jit(solution)/shard_map/gram/reduce_sum | solution.py:256
  119.4 0.0 all-gather.2.cloned.1.call-update
  119.4 75.2 %conditional.3 = (f32[4096,128]{1,0:T(8,128)S(1)}) conditional(s32[]{:T(128)} %convert_element_type.4, f32[4096,128]{1,0:T(8,128)S(1)} %add.6, f32[4096,128]{1,0:T(8,128)S(1)} %add.6), branch_computations={%region_3.0_spmd, %region_4.0_spmd} | conditional | flops 516096 | bytes 12648460 | solution.py:295
  119.4 35.7 %all_to_all.33 = f32[128,32,128]{2,1,0:T(8,128)} all-to-all(f32[128,32,128]{2,1,0:T(8,128)S(1)} %bitcast.18), channel_id=1, replica_groups=mesh['row'=16,'col'=8] {'row','col'}, dimensions={0} | all-to-all | bytes 4194304 | tf_op jit(solution)/shard_map/cond/branch_1_fun/proj/all_to_all | solution.py:252
  155.1 1.7 reduce_sum.16
  156.9 0.2 broadcast_in_dim.0
  157.1 37.5 %all_to_all.34 = f32[128,32,128]{2,1,0:T(8,128)S(1)} all-to-all(f32[128,32,128]{2,1,0:T(8,128)S(1)} %bitcast.20), channel_id=1, replica_groups=mesh['row'=16,'col'=8] {'row','col'}, dimensions={0} | all-to-all | bytes 4194304 | tf_op jit(solution)/shard_map/cond/branch_1_fun/proj/all_to_all | solution.py:252
  194.7 25.0 %all-gather.2.cloned.1.call-done = f32[14336,128]{1,0:T(8,128)} async-done(((f32[112,128]{1,0:T(8,128)}), f32[14336,128]{1,0:T(8,128)}) %all-gather.2.cloned.1.call-update) | async-done | bytes 7340048 | tf_op jit(solution)/shard_map/gram/all_gather | solution.py:287
  219.6 10.8 %solve.1.c_ref = f32[4096,128]{1,0:T(8,128)} custom-call(f32[4096,128]{1,0:T(8,128)S(1)} %get-tuple-element.34.p_ref, f32[128,14,8,128]{3,2,1,0:T(8,128)} %bitcast.24, f32[8,256,256]{2,1,0:T(8,128)} %tri_ref.1), custom_call_target="tpu_custom_call" | custom-call | flops 4000000000 | bytes 13000000 | tf_op jit(solution)/shard_map/solve/solve/pallas_call | solution.py:174
  230.4 0.2 collective-permute-start.2
  230.7 11.1 %update.2.rest_0_ = f32[1536,512]{1,0:T(8,128)} custom-call(s32[1]{0:T(128)} %bitcast.5.core_ref.half_ref, f32[4096,128]{1,0:T(8,128)} %solve.1.c_ref, f32[128,4,1536]{2,1,0:T(4,128)} %copy-done, f32[8,1536,256]{2,1,0:T(8,128)} %h_ref.9), custom_call_target="tpu_custom_call" | custom-call | flops 4831838208 | bytes 18000000 | tf_op jit(solution)/shard_map/update/update/pallas_call | solution.py:227
  241.8 0.0 collective-permute-done.2.c_ref
  241.8 0.0 copy-start.1
  241.8 1.3 copy-done.1
  243.1 11.1 %update.3 = f32[1536,512]{1,0:T(8,128)} custom-call(s32[1]{0:T(128)S(6)} %sub.3.half_ref, f32[4096,128]{1,0:T(8,128)} %copy-done.1, f32[128,4,1536]{2,1,0:T(4,128)} %copy-done, f32[8,1536,256]{2,1,0:T(8,128)} %h_ref.9, f32[1536,512]{1,0:T(8,128)} %update.2.rest_0_), custom_call_target="tpu_custom_call", output_to_operand_aliasing={{}: (4, {})} | custom-call | flops 4831838208 | bytes 18000000 | tf_op jit(solution)/shard_map/update/update/pallas_call | solution.py:227
Async XLA Ops:
  6.5 53.3 %all-to-all-start.2 = ((f32[128,4,1536]{2,1,0:T(4,128)}), f32[128,4,1536]{2,1,0:T(4,128)S(1)}, u32[]{:S(2)}, u32[]{:S(2)}) async-start(f32[128,4,1536]{2,1,0:T(4,128)} %bitcast.22), calls=%async_computation.2 | async-start | bytes 6291456 | tf_op jit(solution)/shard_map/rows/all_to_all | solution.py:252
  46.6 7.3 %collective-permute-start = (f32[7168,128]{1,0:T(8,128)}, f32[7168,128]{1,0:T(8,128)S(1)}, u32[]{:S(2)}, u32[]{:S(2)}) collective-permute-start(f32[7168,128]{1,0:T(8,128)} %bitcast.25), channel_id=1, source_target_pairs={{0,1},{1,0},{2,3},{3,2},{4,5},{5,4},{6,7},{7,6},{8,9},{9,8},{10,11... | collective-permute-start | bytes 11010056 | tf_op jit(solution)/shard_map/gram/cond/branch_1_fun/ppermute | solution.py:248
  59.9 1.7 copy-start
  61.6 55.0 %all-to-all-start.3 = ((f32[128,56,128]{2,1,0:T(8,128)}), f32[128,56,128]{2,1,0:T(8,128)}, u32[]{:S(2)}, u32[]{:S(2)}) async-start(f32[128,56,128]{2,1,0:T(8,128)} %bitcast.17), calls=%async_computation.3 | async-start | bytes 7340032 | tf_op jit(solution)/shard_map/gram/all_to_all | solution.py:252
  69.3 150.3 %all-gather.2.cloned.1.call-start = ((), (), s32[]{:S(2)}) async-start(), calls=%async_computation.4 | async-start | bytes 7397376 | tf_op jit(solution)/shard_map/gram/all_gather | solution.py:287
  81.9 13.6 %collective-permute-start.1 = (f32[4096,128]{1,0:T(8,128)}, f32[4096,128]{1,0:T(8,128)S(1)}, u32[]{:S(2)}, u32[]{:S(2)}) collective-permute-start(f32[4096,128]{1,0:T(8,128)} %proj.3), channel_id=1, source_target_pairs={{0,1},{1,0},{2,3},{3,2},{4,5},{5,4},{6,7},{7,6},{8,9},{9,8},{10,11... | collective-permute-start | bytes 6291464 | tf_op jit(solution)/shard_map/proj/ppermute | solution.py:248
  230.4 11.3 %collective-permute-start.2 = (f32[4096,128]{1,0:T(8,128)}, f32[4096,128]{1,0:T(8,128)S(1)}, u32[]{:S(2)}, u32[]{:S(2)}) collective-permute-start(f32[4096,128]{1,0:T(8,128)} %solve.1.c_ref), channel_id=1, source_target_pairs={{0,1},{1,0},{2,3},{3,2},{4,5},{5,4},{6,7},{7,6},{8,9},{9,8},{10,11... | collective-permute-start | bytes 6291464 | tf_op jit(solution)/shard_map/solve/ppermute | solution.py:248
  241.8 1.3 copy-start.1
Sparse Core Ops, SparseCore 0:
  119.5 100.0 all-gather.1

commit v3 on v2

--- a/solution.py
+++ b/solution.py
@@ -12,7 +12,7 @@
 AXES = ("row", "col")
 NN = ((1,), (0,))
 NT = ((1,), (1,))
-LIMIT = 56 * 1024 * 1024
+MIB = 1024 * 1024
 
 
 def split(x):
@@ -83,7 +83,7 @@
             ],
         ),
         out_shape=[out, out],
-        compiler_params=pltpu.CompilerParams(vmem_limit_bytes=LIMIT),
+        compiler_params=pltpu.CompilerParams(vmem_limit_bytes=40 * MIB),
         cost_estimate=pl.CostEstimate(flops=12 * pairs * rows * width * width, bytes_accessed=20_000_000, transcendentals=0),
         name="gram",
     )(core, house)
@@ -94,7 +94,8 @@
     return x_ref[:, :, pl.ds(at, 128)].reshape(-1, 128)
 
 
-def proj_kernel(half_ref, x_ref, h_ref, out_ref, eh, el):
+def proj_kernel(half_ref, x_ref, h_ref, out_ref, e_ref, *rest):
+    eh, el = rest[-2:]
     b = pl.program_id(0)
     steps = h_ref.shape[1] // 128
     groups = out_ref.shape[0] // eh.shape[0]
@@ -102,22 +103,30 @@
     @pl.when(b == 0)
     def _():
         for t in range(steps):
-            high, low = split(unpack(x_ref, t))
-            eh[:, t * 128:(t + 1) * 128] = high
-            el[:, t * 128:(t + 1) * 128] = low
+            at = slice(t * 128, (t + 1) * 128)
+            e = unpack(x_ref, t)
+            high, low = split(e)
+            eh[:, at] = high
+            el[:, at] = low
+            e_ref[at, :] = e.T
 
     high, low = split(h_ref[0])
+    if len(rest) > 2:
+        rest[0][0] = high
+        rest[1][0] = low
     p = dot3(eh[...], el[...], high, low)
     n = p.shape[0]
     out_ref[pl.ds(2 * b, n, stride=groups), :] = p[:, :128]
     out_ref[pl.ds(2 * b + 1, n, stride=groups), :] = p[:, 128:]
 
 
-def proj_call(half, x, house):
+def proj_call(half, x, house, keep_terms):
     blocks, rows, width = house.shape
     sources, cols = x.shape[0] // 2, x.shape[1]
     n = sources * cols
     groups = blocks * width // 128
+    one = lambda b, h: (b, 0, 0)
+    terms = 2 if keep_terms else 0
     return pl.pallas_call(
         proj_kernel,
         grid_spec=pltpu.PrefetchScalarGridSpec(
@@ -125,16 +134,15 @@
             grid=(blocks,),
             in_specs=[
                 pl.BlockSpec((sources, cols, rows), lambda b, h: (h[0], 0, 0)),
-                pl.BlockSpec((1, rows, width), lambda b, h: (b, 0, 0)),
+                pl.BlockSpec((1, rows, width), one),
             ],
-            out_specs=pl.BlockSpec((n * groups, 128), lambda b, h: (0, 0)),
-            scratch_shapes=[
-                pltpu.VMEM((n, rows), BF),
-                pltpu.VMEM((n, rows), BF),
-            ],
+            out_specs=[pl.BlockSpec((n * groups, 128), lambda b, h: (0, 0)), pl.BlockSpec((rows, n), lambda b, h: (0, 0))]
+            + [pl.BlockSpec((1, rows, width), one)] * terms,
+            scratch_shapes=[pltpu.VMEM((n, rows), BF), pltpu.VMEM((n, rows), BF)],
         ),
-        out_shape=jax.ShapeDtypeStruct((n * groups, 128), F32),
-        compiler_params=pltpu.CompilerParams(vmem_limit_bytes=LIMIT),
+        out_shape=[jax.ShapeDtypeStruct((n * groups, 128), F32), jax.ShapeDtypeStruct((rows, n), F32)]
+        + [jax.ShapeDtypeStruct(house.shape, BF)] * terms,
+        compiler_params=pltpu.CompilerParams(vmem_limit_bytes=28 * MIB),
         cost_estimate=pl.CostEstimate(flops=6 * blocks * n * rows * width, bytes_accessed=16_000_000, transcendentals=0),
         name="proj",
     )(half, x, house)
@@ -163,8 +171,7 @@
         own = slice(b * width, (b + 1) * width)
         ch[:, own] = high
         cl[:, own] = low
-        out_ref[pl.ds(2 * b, n, stride=groups), :] = coef[:, :128]
-        out_ref[pl.ds(2 * b + 1, n, stride=groups), :] = coef[:, 128:]
+        out_ref[b] = coef
 
 
 def solve_call(p, gram, tri):
@@ -175,55 +182,48 @@
         solve_kernel,
         in_specs=[vmem, vmem, vmem],
         out_specs=vmem,
-        out_shape=jax.ShapeDtypeStruct(p.shape, F32),
+        out_shape=jax.ShapeDtypeStruct((blocks, n, width), F32),
         scratch_shapes=[pltpu.VMEM((n, blocks * width), BF), pltpu.VMEM((n, blocks * width), BF)],
-        compiler_params=pltpu.CompilerParams(vmem_limit_bytes=LIMIT),
+        compiler_params=pltpu.CompilerParams(vmem_limit_bytes=24 * MIB),
         cost_estimate=pl.CostEstimate(flops=4_000_000_000, bytes_accessed=13_000_000, transcendentals=0),
         name="solve",
     )(p, gram, tri)
 
 
-def update_kernel(half_ref, c_ref, x_ref, h_ref, *rest):
+def update_kernel(half_ref, c_ref, e_ref, hh_ref, hl_ref, *rest):
     out_ref, ch, cl = rest[-3:]
-    r = pl.program_id(0)
-    blocks, tile, width = h_ref.shape
-    groups = blocks * width // 128
-    n = c_ref.shape[0] // groups
-    here = tile // 128
-
-    @pl.when(r == 0)
+    blocks = hh_ref.shape[0]
+
+    @pl.when(pl.program_id(0) == 0)
     def _():
-        for g in range(groups):
-            high, low = split(c_ref[pl.ds(g, n, stride=groups), :].T)
-            ch[g * 128:(g + 1) * 128, :] = high
-            cl[g * 128:(g + 1) * 128, :] = low
-
-    total = jnp.zeros((tile, n), F32)
+        for b in range(blocks):
+            high, low = split(c_ref[b])
+            ch[b] = high
+            cl[b] = low
+
+    total = e_ref[...]
     for b in range(blocks):
-        high, low = split(h_ref[b])
-        at = slice(b * width, (b + 1) * width)
-        total = total + dot3(high, low, ch[at, :], cl[at, :])
-    for t in range(here):
-        e = unpack(x_ref, r * here + t)
-        out_ref[t * 128:(t + 1) * 128, :] = e.T - total[t * 128:(t + 1) * 128, :]
-
-
-def update_call(half, coef, x, house, prev, tile=512):
-    blocks, rows, width = house.shape
-    sources, cols = x.shape[0] // 2, x.shape[1]
-    n = sources * cols
-    whole = lambda r, h: (0, 0)
+        high = hh_ref[b]
+        total = total - (dot(high, ch[b], NT) + (dot(high, cl[b], NT) + dot(hl_ref[b], ch[b], NT)))
+    out_ref[...] = total
+
+
+def update_call(half, coef, e, terms, prev, tile=512):
+    blocks, rows, width = terms[0].shape
+    n = e.shape[1]
+    piece = pl.BlockSpec((blocks, tile, width), lambda r, h: (0, r, 0))
     in_specs = [
-        pl.BlockSpec(coef.shape, whole),
-        pl.BlockSpec((sources, cols, rows), lambda r, h: (h[0], 0, 0)),
-        pl.BlockSpec((blocks, tile, width), lambda r, h: (0, r, 0)),
+        pl.BlockSpec(coef.shape, lambda r, h: (0, 0, 0)),
+        pl.BlockSpec((tile, n), lambda r, h: (r, 0)),
+        piece,
+        piece,
     ]
-    args = [half, coef, x, house]
+    args = [half, coef, e, *terms]
     aliases = {}
     if prev is not None:
         in_specs.append(pl.BlockSpec(memory_space=pl.ANY))
         args.append(prev)
-        aliases = {4: 0}
+        aliases = {5: 0}
     return pl.pallas_call(
         update_kernel,
         grid_spec=pltpu.PrefetchScalarGridSpec(
@@ -231,14 +231,11 @@
             grid=(rows // tile,),
             in_specs=in_specs,
             out_specs=pl.BlockSpec((tile, n), lambda r, h: (r, h[0])),
-            scratch_shapes=[
-                pltpu.VMEM((blocks * width, n), BF),
-                pltpu.VMEM((blocks * width, n), BF),
-            ],
+            scratch_shapes=[pltpu.VMEM(coef.shape, BF), pltpu.VMEM(coef.shape, BF)],
         ),
         out_shape=jax.ShapeDtypeStruct((rows, 2 * n), F32),
         input_output_aliases=aliases,
-        compiler_params=pltpu.CompilerParams(vmem_limit_bytes=LIMIT),
+        compiler_params=pltpu.CompilerParams(vmem_limit_bytes=24 * MIB),
         cost_estimate=pl.CostEstimate(flops=6 * blocks * n * rows * width, bytes_accessed=18_000_000, transcendentals=0),
         name="update",
     )(*args)
@@ -279,8 +276,10 @@
         keep = lax.cond(always, lambda keep, send: keep + pair_swap(send), lambda keep, send: keep, keep, send)
         got = all_to_all(after(keep, x))
     with jax.named_scope("proj"):
-        send = pair_swap(proj_call(away, x, house))
-        proj = proj_call(core, x, house) + send
+        send, e_far = proj_call(away, x, house, False)
+        send = pair_swap(send)
+        proj, e_near, *terms = proj_call(core, x, house, True)
+        proj = proj + send
     with jax.named_scope("gram"):
         got, proj = lax.optimization_barrier((got, proj))
         share = sums(got, devices)
@@ -297,8 +296,8 @@
         near = solve_call(proj, gram, tri)
         far = pair_swap(near)
     with jax.named_scope("update"):
-        out = update_call(core, near, x, house, None)
-        out = update_call(away, far, x, house, out)
+        out = update_call(core, near, e_near, terms, None)
+        out = update_call(away, far, e_far, terms, out)
     return out
 
 

time: 262 us -> 260 us (level)
  local copies, waits for them, and re-layouts: 3.29 us -> 24.5 us
  Pallas kernels: 86.5 us -> 67.2 us
  waiting for transfers between devices: 52.2 us -> 45.4 us
    unnamed x4 -> x26, local copies, waits for them, and re-layouts: 3.04 us -> 24.3 us
    pallas_call x2, Pallas kernels: 22.2 us -> 15 us  [update_call(): pl.pallas_call(update_kernel, grid_spec=pltpu.PrefetchScalarGridSpec(num_...]
    pallas_call x2, Pallas kernels: 25 us -> 18 us  [proj_call(): pl.pallas_call(proj_kernel, grid_spec=pltpu.PrefetchScalarGridSpec(num_sc...]
    all_to_all x2, waiting for transfers between devices: 21 us -> 14.1 us  [all_to_all(): return lax.all_to_all(x, AXES, 0, 0, tiled=True)]
    pallas_call x1, Pallas kernels: 10.8 us -> 7.12 us  [solve_call(): pl.pallas_call(solve_kernel, in_specs=[vmem, vmem, vmem], out_specs=vmem,...]
  transfers between devices with their start and end apart: 6 -> 6, of which waited for: 4 -> 3; matrix products, arithmetic and copies ran while one was open for 3% -> 3% of each run, Pallas kernels for 25% -> 20%
where the time goes in v3:
time: 260 us
  blocking collectives  74.9 us (29%)
  Pallas kernels  67.2 us (26%)
  waiting for transfers between devices  45.4 us (17%)
  local copies, waits for them, and re-layouts  24.5 us (9%)
  starting transfers between devices  23.7 us (9%)
  between operations  13.5 us (5%)
  other arithmetic  10.5 us (4%)
    all_to_all x2, blocking collectives, all_to_all(): return lax.all_to_all(x, AXES, 0, 0, tiled=True)  74.9 us
    pallas_call x1, Pallas kernels, gram_call(): pl.pallas_call(gram_kernel, grid_spec=pltpu.PrefetchScalarGridSpec(num_sc...  27.1 us
    all_gather x1, waiting for transfers between devices, local(): gram = lax.all_gather(share.reshape(-1, 128), AXES, axis=0, tiled=True)  25 us
    unnamed x26, local copies, waits for them, and re-layouts  24.3 us
    all_to_all x2, starting transfers between devices, all_to_all(): return lax.all_to_all(x, AXES, 0, 0, tiled=True)  21 us
    pallas_call x2, Pallas kernels, proj_call(): pl.pallas_call(proj_kernel, grid_spec=pltpu.PrefetchScalarGridSpec(num_sc...  18 us
    pallas_call x2, Pallas kernels, update_call(): pl.pallas_call(update_kernel, grid_spec=pltpu.PrefetchScalarGridSpec(num_...  15 us
    all_to_all x2, waiting for transfers between devices, all_to_all(): return lax.all_to_all(x, AXES, 0, 0, tiled=True)  14.1 us
  transfers between devices with their start and end apart: 6, of which 3 were waited for; matrix products, arithmetic and copies ran while one was open for 3% of the time, Pallas kernels for 20%

profile of v3, /device:TPU:1, one launch (start us, length us, event | category | flops | bytes accessed | tf_op | source)
XLA Modules:
  0.0 259.7 jit_solution(17776836302201653284)
XLA Ops:
  6.5 11.5 %all-to-all-start.2 = ((f32[128,4,1536]{2,1,0:T(4,128)}), f32[128,4,1536]{2,1,0:T(4,128)S(1)}, u32[]{:S(2)}, u32[]{:S(2)}) async-start(f32[128,4,1536]{2,1,0:T(4,128)} %bitcast.25), calls=%async_computation.2 | async-start | bytes 6291456 | tf_op jit(solution)/shard_map/rows/all_to_all | solution.py:249
  18.1 4.6 %copy-done.7 = f32[8,1536,256]{2,1,0:T(8,128)S(1)} copy-done((f32[8,1536,256]{2,1,0:T(8,128)S(1)}, f32[8,1536,256]{2,1,0:T(8,128)}, u32[]{:S(2)}) %copy-start.7) | copy-done | bytes 12582936
  22.6 27.1 %gram.1 = (f32[128,7,8,128]{3,2,1,0:T(8,128)}, f32[128,7,8,128]{3,2,1,0:T(8,128)}) custom-call(s32[1]{0:T(128)} %bitcast.5.core_ref.half_ref, f32[8,1536,256]{2,1,0:T(8,128)S(1)} %copy-done.7), custom_call_target="tpu_custom_call" | custom-call | flops 33822867456 | bytes 20000000 | tf_op jit(solution)/shard_map/gram/gram/pallas_call | solution.py:71
  49.7 11.6 %conditional.2 = (f32[7168,128]{1,0:T(8,128)}) conditional(s32[]{:T(128)} %convert_element_type.4, f32[7168,128]{1,0:T(8,128)} %bitcast.18, (f32[128,7,8,128]{3,2,1,0:T(8,128)}, f32[7168,128]{1,0:T(8,128)}) %tuple.30), branch_computations={%region_0.0_spmd, %region_1.0_spmd} | conditional | flops 917504 | bytes 25690160 | solution.py:276
  49.7 1.1 collective-permute-start
  50.8 6.2 %collective-permute-done = f32[7168,128]{1,0:T(8,128)S(1)} collective-permute-done((f32[7168,128]{1,0:T(8,128)}, f32[7168,128]{1,0:T(8,128)S(1)}, u32[]{:S(2)}, u32[]{:S(2)}) %collective-permute-start) | collective-permute-done | bytes 3670048 | tf_op jit(solution)/shard_map/gram/cond/branch_1_fun/ppermute | solution.py:245
  57.0 4.2 %add.4 = f32[7168,128]{1,0:T(8,128)} add(f32[7168,128]{1,0:T(8,128)} %get-tuple-element.19, f32[7168,128]{1,0:T(8,128)S(1)} %collective-permute-done) | non-fusion elementwise | flops 917504 | bytes 11010048 | tf_op jit(solution)/shard_map/gram/cond/branch_1_fun/add | solution.py:276
  61.3 9.5 %all-to-all-start.3 = ((f32[128,56,128]{2,1,0:T(8,128)}), f32[128,56,128]{2,1,0:T(8,128)}, u32[]{:S(2)}, u32[]{:S(2)}) async-start(f32[128,56,128]{2,1,0:T(8,128)} %bitcast.20), calls=%async_computation.3 | async-start | bytes 7340032 | tf_op jit(solution)/shard_map/gram/all_to_all | solution.py:249
  70.8 4.6 %copy-done.8 = f32[8,1536,256]{2,1,0:T(8,128)S(1)} copy-done((f32[8,1536,256]{2,1,0:T(8,128)S(1)}, f32[8,1536,256]{2,1,0:T(8,128)}, u32[]{:S(2)}) %copy-start.8) | copy-done | bytes 12582936
  75.4 7.2 %proj.3 = (f32[4096,128]{1,0:T(8,128)S(1)}, f32[1536,256]{1,0:T(8,128)S(1)}) custom-call(s32[1]{0:T(128)S(6)} %sub.3.half_ref, f32[128,4,1536]{2,1,0:T(4,128)S(1)} %all-to-all-done.2.x_ref, f32[8,1536,256]{2,1,0:T(8,128)S(1)} %copy-done.8), custom_call_target="tpu_custom_call" | custom-call | flops 4831838208 | bytes 16000000 | tf_op jit(solution)/shard_map/proj/proj/pallas_call | solution.py:130
  82.6 1.2 copy-done.3
  83.8 1.1 collective-permute-start.1
  85.0 10.8 %proj.2 = (f32[4096,128]{1,0:T(8,128)S(1)}, f32[1536,256]{1,0:T(8,128)S(1)}, bf16[8,1536,256]{2,1,0:T(8,128)(2,1)S(1)}, bf16[8,1536,256]{2,1,0:T(8,128)(2,1)S(1)}) custom-call(s32[1]{0:T(128)} %bitcast.5.core_ref.half_ref, f32[128,4,1536]{2,1,0:T(4,128)S(1)} %all-to-all-done.2.x_ref, f32[8,1536,256]{2,1,0:T(8,128)} %h_ref.5), custom_call_target="tpu_custom_call" | custom-call | flops 4831838208 | bytes 16000000 | tf_op jit(solution)/shard_map/proj/proj/pallas_call | solution.py:130
  95.8 2.7 %copy-done = bf16[8,1536,256]{2,1,0:T(8,128)(2,1)} copy-done((bf16[8,1536,256]{2,1,0:T(8,128)(2,1)}, bf16[8,1536,256]{2,1,0:T(8,128)(2,1)S(1)}, u32[]{:S(2)}) %copy-start) | copy-done | bytes 6291480
  98.5 2.6 copy-done.1
  101.0 1.1 copy-done.5
  102.2 1.7 add.6
  103.9 14.1 %all-to-all-done.3 = f32[128,56,128]{2,1,0:T(8,128)} async-done(((f32[128,56,128]{2,1,0:T(8,128)}), f32[128,56,128]{2,1,0:T(8,128)}, u32[]{:S(2)}, u32[]{:S(2)}) %all-to-all-start.3) | async-done | bytes 3670048 | tf_op jit(solution)/shard_map/gram/all_to_all | solution.py:249
  118.0 2.8 %reduce_sum.18 = f32[2,56,128]{2,1,0:T(8,128)} reduce(f32[64,2,56,128]{3,2,1,0:T(8,128)} %bitcast.11, f32[]{:T(128)} %constant.15.clone.1), dimensions={0}, to_apply=%region_2.0 | reduce | flops 903168 | bytes 3727364 | tf_op jit(solution)/shard_map/gram/reduce_sum | solution.py:253
  120.9 76.9 %conditional.3 = (f32[4096,128]{1,0:T(8,128)}) conditional(s32[]{:T(128)} %convert_element_type.4, f32[4096,128]{1,0:T(8,128)} %add.6, f32[4096,128]{1,0:T(8,128)} %add.6), branch_computations={%region_3.0_spmd, %region_4.0_spmd} | conditional | flops 516096 | bytes 12648460 | solution.py:294
  120.9 36.8 %all_to_all.33 = f32[128,32,128]{2,1,0:T(8,128)} all-to-all(f32[128,32,128]{2,1,0:T(8,128)} %bitcast.21), channel_id=1, replica_groups=mesh['row'=16,'col'=8] {'row','col'}, dimensions={0} | all-to-all | bytes 4194304 | tf_op jit(solution)/shard_map/cond/branch_1_fun/proj/all_to_all | solution.py:249
  157.7 1.7 reduce_sum.16
  159.4 0.2 broadcast_in_dim.0
  159.7 38.1 %all_to_all.34 = f32[128,32,128]{2,1,0:T(8,128)} all-to-all(f32[128,32,128]{2,1,0:T(8,128)S(1)} %bitcast.23), channel_id=1, replica_groups=mesh['row'=16,'col'=8] {'row','col'}, dimensions={0} | all-to-all | bytes 4194304 | tf_op jit(solution)/shard_map/cond/branch_1_fun/proj/all_to_all | solution.py:249
  197.7 25.0 %all-gather.2.cloned.1.call-done = f32[14336,128]{1,0:T(8,128)} async-done(((f32[112,128]{1,0:T(8,128)}), f32[14336,128]{1,0:T(8,128)}) %all-gather.2.cloned.1.call-update) | async-done | bytes 7340048 | tf_op jit(solution)/shard_map/gram/all_gather | solution.py:286
  222.7 3.1 %copy-done.9 = f32[14336,128]{1,0:T(8,128)S(1)} copy-done((f32[14336,128]{1,0:T(8,128)S(1)}, f32[14336,128]{1,0:T(8,128)}, u32[]{:S(2)}) %copy-start.9) | copy-done | bytes 7340056
  225.8 1.6 copy-done.10
  227.4 7.1 %solve.1.c_ref = f32[8,256,256]{2,1,0:T(8,128)S(1)} custom-call(f32[4096,128]{1,0:T(8,128)} %get-tuple-element.46.p_ref, f32[128,14,8,128]{3,2,1,0:T(8,128)S(1)} %bitcast.17, f32[8,256,256]{2,1,0:T(8,128)S(1)} %copy-done.10), custom_call_target="tpu_custom_call" | custom-call | flops 4000000000 | bytes 13000000 | tf_op jit(solution)/shard_map/solve/solve/pallas_call | solution.py:181
  234.5 0.5 collective-permute-start.2
  235.1 2.8 %copy-done.2 = bf16[8,1536,256]{2,1,0:T(8,128)(2,1)S(1)} copy-done((bf16[8,1536,256]{2,1,0:T(8,128)(2,1)S(1)}, bf16[8,1536,256]{2,1,0:T(8,128)(2,1)}, u32[]{:S(2)}) %copy-start.2) | copy-done | bytes 6291480
  237.9 7.5 %update.2.rest_0_ = f32[1536,512]{1,0:T(8,128)} custom-call(s32[1]{0:T(128)} %bitcast.5.core_ref.half_ref, f32[8,256,256]{2,1,0:T(8,128)S(1)} %solve.1.c_ref, f32[1536,256]{1,0:T(8,128)S(1)} %copy-done.6, bf16[8,1536,256]{2,1,0:T(8,128)(2,1)S(1)} %bitcast.16, bf16[8,1536,256]{2,1,0:T(8,128)(2,1)S(1)} %copy-done.2), custom_call_target="tpu_custom_call" | custom-call | flops 4831838208 | bytes 18000000 | tf_op jit(solution)/shard_map/update/update/pallas_call | solution.py:227
  245.4 7.5 %update.3 = f32[1536,512]{1,0:T(8,128)} custom-call(s32[1]{0:T(128)S(6)} %sub.3.half_ref, f32[8,256,256]{2,1,0:T(8,128)S(1)} %collective-permute-done.2.c_ref, f32[1536,256]{1,0:T(8,128)S(1)} %copy-done.4, bf16[8,1536,256]{2,1,0:T(8,128)(2,1)S(1)} %bitcast.16, bf16[8,1536,256]{2,1,0:T(8,128)(2,1)S(1)} %copy-done.2, ...), custom_call_target="tpu_custom_call", output_to_operand_aliasing={{}: (5, {})} | custom-call | flops 4831838208 | bytes 18000000 | tf_op jit(solution)/shard_map/update/update/pallas_call | solution.py:227
  (23 shorter events, 0.1 us)
Async XLA Ops:
  6.5 54.8 %all-to-all-start.2 = ((f32[128,4,1536]{2,1,0:T(4,128)}), f32[128,4,1536]{2,1,0:T(4,128)S(1)}, u32[]{:S(2)}, u32[]{:S(2)}) async-start(f32[128,4,1536]{2,1,0:T(4,128)} %bitcast.25), calls=%async_computation.2 | async-start | bytes 6291456 | tf_op jit(solution)/shard_map/rows/all_to_all | solution.py:249
  18.0 4.6 %copy-start.7 = (f32[8,1536,256]{2,1,0:T(8,128)S(1)}, f32[8,1536,256]{2,1,0:T(8,128)}, u32[]{:S(2)}) copy-start(f32[8,1536,256]{2,1,0:T(8,128)} %h_ref.5) | copy-start | bytes 37748740
  49.7 7.3 %collective-permute-start = (f32[7168,128]{1,0:T(8,128)}, f32[7168,128]{1,0:T(8,128)S(1)}, u32[]{:S(2)}, u32[]{:S(2)}) collective-permute-start(f32[7168,128]{1,0:T(8,128)} %bitcast.27), channel_id=1, source_target_pairs={{0,1},{1,0},{2,3},{3,2},{4,5},{5,4},{6,7},{7,6},{8,9},{9,8},{10,11... | collective-permute-start | bytes 11010056 | tf_op jit(solution)/shard_map/gram/cond/branch_1_fun/ppermute | solution.py:245
  61.3 56.7 %all-to-all-start.3 = ((f32[128,56,128]{2,1,0:T(8,128)}), f32[128,56,128]{2,1,0:T(8,128)}, u32[]{:S(2)}, u32[]{:S(2)}) async-start(f32[128,56,128]{2,1,0:T(8,128)} %bitcast.20), calls=%async_computation.3 | async-start | bytes 7340032 | tf_op jit(solution)/shard_map/gram/all_to_all | solution.py:249
  70.8 152.0 %all-gather.2.cloned.1.call-start = ((), (), s32[]{:S(2)}) async-start(), calls=%async_computation.4 | async-start | bytes 7397376 | tf_op jit(solution)/shard_map/gram/all_gather | solution.py:286
  70.8 4.6 %copy-start.8 = (f32[8,1536,256]{2,1,0:T(8,128)S(1)}, f32[8,1536,256]{2,1,0:T(8,128)}, u32[]{:S(2)}) copy-start(f32[8,1536,256]{2,1,0:T(8,128)} %h_ref.5) | copy-start | bytes 37748740
  82.6 1.2 copy-start.3
  83.8 18.4 %collective-permute-start.1 = (f32[4096,128]{1,0:T(8,128)S(1)}, f32[4096,128]{1,0:T(8,128)S(1)}, u32[]{:S(2)}, u32[]{:S(2)}) collective-permute-start(f32[4096,128]{1,0:T(8,128)S(1)} %get-tuple-element.37), channel_id=1, source_target_pairs={{0,1},{1,0},{2,3},{3,2},{4,5},{5,4},{6,7},{7,6},{8,9},{9,8},{10,11... | collective-permute-start | bytes 6291464 | tf_op jit(solution)/shard_map/proj/ppermute | solution.py:245
  95.7 2.7 %copy-start = (bf16[8,1536,256]{2,1,0:T(8,128)(2,1)}, bf16[8,1536,256]{2,1,0:T(8,128)(2,1)S(1)}, u32[]{:S(2)}) copy-start(bf16[8,1536,256]{2,1,0:T(8,128)(2,1)S(1)} %get-tuple-element.42.hh_ref) | copy-start | bytes 18874372
  98.5 2.6 copy-start.1
  101.0 1.1 copy-start.5
  120.9 114.2 %slice-start = ((s8[6291456]{0:T(1024)(128)(4,1)}), s8[2097152]{0:T(1024)(128)(4,1)S(1)}, s32[]{:S(2)}) async-start(s8[6291456]{0:T(1024)(128)(4,1)} %bitcast.15), calls=%async_computation.5 | async-start | bytes 4194304
  222.7 3.1 %copy-start.9 = (f32[14336,128]{1,0:T(8,128)S(1)}, f32[14336,128]{1,0:T(8,128)}, u32[]{:S(2)}) copy-start(f32[14336,128]{1,0:T(8,128)} %all-gather.2.cloned.1.call-done) | copy-start | bytes 22020100
  225.8 1.6 copy-start.10
  227.4 7.7 %slice-start.1 = ((s8[6291456]{0:T(1024)(128)(4,1)}), s8[4194304]{0:T(1024)(128)(4,1)S(1)}, s32[]{:S(2)}) async-start(s8[6291456]{0:T(1024)(128)(4,1)} %bitcast.15), calls=%async_computation.6 | async-start | bytes 8388608
  227.4 7.7 %copy-start.6 = (f32[1536,256]{1,0:T(8,128)S(1)}, f32[1536,256]{1,0:T(8,128)}, u32[]{:S(2)}) copy-start(f32[1536,256]{1,0:T(8,128)} %copy-done.5) | copy-start | bytes 4718596
  234.5 10.8 %collective-permute-start.2 = (f32[8,256,256]{2,1,0:T(8,128)S(1)}, f32[8,256,256]{2,1,0:T(8,128)S(1)}, u32[]{:S(2)}, u32[]{:S(2)}) collective-permute-start(f32[8,256,256]{2,1,0:T(8,128)S(1)} %solve.1.c_ref), channel_id=1, source_target_pairs={{0,1},{1,0},{2,3},{3,2},{4,5},{5,4},{6,7},{7,6},{8,9},{9,8},{10,11... | collective-permute-start | bytes 6291464 | tf_op jit(solution)/shard_map/solve/ppermute | solution.py:245
  235.1 2.8 %copy-start.2 = (bf16[8,1536,256]{2,1,0:T(8,128)(2,1)S(1)}, bf16[8,1536,256]{2,1,0:T(8,128)(2,1)}, u32[]{:S(2)}) copy-start(bf16[8,1536,256]{2,1,0:T(8,128)(2,1)} %copy-done.1) | copy-start | bytes 18874372
  237.9 7.5 %copy-start.4 = (f32[1536,256]{1,0:T(8,128)S(1)}, f32[1536,256]{1,0:T(8,128)}, u32[]{:S(2)}) copy-start(f32[1536,256]{1,0:T(8,128)} %copy-done.3) | copy-start | bytes 4718596
Sparse Core Ops, SparseCore 0:
  121.0 101.6 all-gather.1

commit v4 on v3

--- a/solution.py
+++ b/solution.py
@@ -148,97 +148,109 @@
     )(half, x, house)
 
 
-def solve_kernel(p_ref, g_ref, tri_ref, out_ref, ch, cl):
-    blocks, width = tri_ref.shape[0], tri_ref.shape[1]
+def finish_kernel(core_ref, near_ref, far_ref, g_ref, tri_ref, e_near_ref, e_far_ref, hh_ref, hl_ref, out_ref,
+                  near, far, g, tri, e_near, e_far, hh, hl, out, ch, cl, sems, t_sems, g_sems, h_sems, out_sems):
+    blocks, width = tri.shape[0], tri.shape[1]
     groups = 2 * blocks
-    n = p_ref.shape[0] // groups
+    n = near.shape[0] // groups
     chunks = width // 8
-    runs = g_ref.shape[0] // chunks
-    deep = g_ref.shape[1] // 2
+    deep = g.shape[1] // 2
+    runs = g.shape[0] // chunks
+    rows = out.shape[0]
+    first_core = core_ref[0] == 0
+    small = [
+        pltpu.make_async_copy(source, target, sems.at[i])
+        for i, (source, target) in enumerate(
+            ((near_ref, near), (far_ref, far), (e_near_ref, e_near), (e_far_ref, e_far))
+        )
+    ]
+    tris = [pltpu.make_async_copy(tri_ref.at[b], tri.at[b], t_sems.at[b]) for b in range(blocks)]
+    parts = [pl.ds(i * chunks, chunks) for i in range(runs)]
+    strips = [pltpu.make_async_copy(g_ref.at[parts[i]], g.at[parts[i]], g_sems.at[i]) for i in range(runs)]
+    terms = [pltpu.make_async_copy(hh_ref.at[b], hh.at[b], h_sems.at[b]) for b in range(blocks)]
+    terms += [pltpu.make_async_copy(hl_ref.at[b], hl.at[b], h_sems.at[blocks + b]) for b in range(blocks)]
+    for copy in small[:2] + tris[:1]:
+        copy.start()
+    for copy in strips[:1] + tris[1:3] + strips[1:] + tris[3:]:
+        copy.start()
+    for copy in small[:2]:
+        copy.wait()
+
+    def columns(ref, b):
+        return jnp.concatenate([ref[2 * b * n:(2 * b + 1) * n, :], ref[(2 * b + 1) * n:(2 * b + 2) * n, :]], axis=1)
+
+    later = small[2:] + terms
     for b in range(blocks):
-        p = jnp.concatenate([p_ref[pl.ds(2 * b, n, stride=groups), :], p_ref[pl.ds(2 * b + 1, n, stride=groups), :]], axis=1)
+        one, two = columns(near, b), columns(far, b)
+        p = jnp.concatenate([jnp.where(first_core, one, two), jnp.where(first_core, two, one)], axis=0)
         for a in range(b):
             pair = b * (b - 1) // 2 + a
-            at = pl.ds(pair % runs * chunks, chunks)
-            g = [g_ref[at, half * deep + pair // runs].reshape(width, 128) for half in range(2)]
-            high, low = split(jnp.concatenate(g, axis=1))
-            own = slice(a * width, (a + 1) * width)
-            p = p - dot3(ch[:, own], cl[:, own], high, low)
+            if pair < runs:
+                strips[pair].wait()
+            block = [g[parts[pair % runs], half * deep + pair // runs].reshape(width, 128) for half in range(2)]
+            high, low = split(jnp.concatenate(block, axis=1))
+            p = p - dot3(ch[a], cl[a], high, low)
         high, low = split(p)
-        t_high, t_low = split(tri_ref[b])
+        tris[b].wait()
+        t_high, t_low = split(tri[b])
         coef = dot(high, t_high, NT) + (dot(high, t_low, NT) + dot(low, t_high, NT))
         high, low = split(coef)
-        own = slice(b * width, (b + 1) * width)
-        ch[:, own] = high
-        cl[:, own] = low
-        out_ref[b] = coef
-
-
-def solve_call(p, gram, tri):
-    blocks, width = tri.shape[0], tri.shape[1]
-    n = p.shape[0] // (2 * blocks)
-    vmem = pl.BlockSpec(memory_space=pltpu.VMEM)
+        ch[b] = high
+        cl[b] = low
+        if b >= 2:
+            for copy in later[(b - 2) * 3:(b - 1) * 3]:
+                copy.start()
+
+    for copy in later:
+        copy.wait()
+    tile = 512
+    sent = []
+    for r in range(rows // tile):
+        at = slice(r * tile, (r + 1) * tile)
+        one, two = e_near[at, :], e_far[at, :]
+        total = jnp.concatenate([jnp.where(first_core, one, two), jnp.where(first_core, two, one)], axis=1)
+        for b in range(blocks):
+            high = hh[b, at, :]
+            total = total - (dot(high, ch[b], NT) + (dot(high, cl[b], NT) + dot(hl[b, at, :], ch[b], NT)))
+        out[at, :] = total
+        sent.append(pltpu.make_async_copy(out.at[at, :], out_ref.at[at, :], out_sems.at[r]))
+        sent[-1].start()
+    for copy in sent:
+        copy.wait()
+
+
+def finish_call(core, near, far, gram, tri, e_near, e_far, terms):
+    blocks, rows, width = terms[0].shape
+    n = e_near.shape[1]
+    anywhere = pl.BlockSpec(memory_space=pl.ANY)
+    dma = pltpu.SemaphoreType.DMA
     return pl.pallas_call(
-        solve_kernel,
-        in_specs=[vmem, vmem, vmem],
-        out_specs=vmem,
-        out_shape=jax.ShapeDtypeStruct((blocks, n, width), F32),
-        scratch_shapes=[pltpu.VMEM((n, blocks * width), BF), pltpu.VMEM((n, blocks * width), BF)],
-        compiler_params=pltpu.CompilerParams(vmem_limit_bytes=24 * MIB),
-        cost_estimate=pl.CostEstimate(flops=4_000_000_000, bytes_accessed=13_000_000, transcendentals=0),
-        name="solve",
-    )(p, gram, tri)
-
-
-def update_kernel(half_ref, c_ref, e_ref, hh_ref, hl_ref, *rest):
-    out_ref, ch, cl = rest[-3:]
-    blocks = hh_ref.shape[0]
-
-    @pl.when(pl.program_id(0) == 0)
-    def _():
-        for b in range(blocks):
-            high, low = split(c_ref[b])
-            ch[b] = high
-            cl[b] = low
-
-    total = e_ref[...]
-    for b in range(blocks):
-        high = hh_ref[b]
-        total = total - (dot(high, ch[b], NT) + (dot(high, cl[b], NT) + dot(hl_ref[b], ch[b], NT)))
-    out_ref[...] = total
-
-
-def update_call(half, coef, e, terms, prev, tile=512):
-    blocks, rows, width = terms[0].shape
-    n = e.shape[1]
-    piece = pl.BlockSpec((blocks, tile, width), lambda r, h: (0, r, 0))
-    in_specs = [
-        pl.BlockSpec(coef.shape, lambda r, h: (0, 0, 0)),
-        pl.BlockSpec((tile, n), lambda r, h: (r, 0)),
-        piece,
-        piece,
-    ]
-    args = [half, coef, e, *terms]
-    aliases = {}
-    if prev is not None:
-        in_specs.append(pl.BlockSpec(memory_space=pl.ANY))
-        args.append(prev)
-        aliases = {5: 0}
-    return pl.pallas_call(
-        update_kernel,
-        grid_spec=pltpu.PrefetchScalarGridSpec(
-            num_scalar_prefetch=1,
-            grid=(rows // tile,),
-            in_specs=in_specs,
-            out_specs=pl.BlockSpec((tile, n), lambda r, h: (r, h[0])),
-            scratch_shapes=[pltpu.VMEM(coef.shape, BF), pltpu.VMEM(coef.shape, BF)],
-        ),
+        finish_kernel,
+        in_specs=[pl.BlockSpec(memory_space=pltpu.SMEM)] + [anywhere] * 8,
+        out_specs=anywhere,
         out_shape=jax.ShapeDtypeStruct((rows, 2 * n), F32),
-        input_output_aliases=aliases,
-        compiler_params=pltpu.CompilerParams(vmem_limit_bytes=24 * MIB),
-        cost_estimate=pl.CostEstimate(flops=6 * blocks * n * rows * width, bytes_accessed=18_000_000, transcendentals=0),
-        name="update",
-    )(*args)
+        scratch_shapes=[
+            pltpu.VMEM(near.shape, F32),
+            pltpu.VMEM(far.shape, F32),
+            pltpu.VMEM(gram.shape, F32),
+            pltpu.VMEM(tri.shape, F32),
+            pltpu.VMEM(e_near.shape, F32),
+            pltpu.VMEM(e_far.shape, F32),
+            pltpu.VMEM(terms[0].shape, BF),
+            pltpu.VMEM(terms[1].shape, BF),
+            pltpu.VMEM((rows, 2 * n), F32),
+            pltpu.VMEM((blocks, 2 * n, width), BF),
+            pltpu.VMEM((blocks, 2 * n, width), BF),
+            dma((4,)),
+            dma((blocks,)),
+            dma((8 * gram.shape[0] // width,)),
+            dma((2 * blocks,)),
+            dma((rows // 512,)),
+        ],
+        compiler_params=pltpu.CompilerParams(vmem_limit_bytes=54 * MIB),
+        cost_estimate=pl.CostEstimate(flops=17_000_000_000, bytes_accessed=35_000_000, transcendentals=0),
+        name="finish",
+    )(core, near, far, gram, tri, e_near, e_far, *terms)
 
 
 def pair_swap(x):
@@ -289,16 +301,13 @@
     def exchange(proj):
         with jax.named_scope("proj"):
             proj = sums(all_to_all(proj), devices)
-            return all_to_all(copies(proj, devices))
-
-    proj = lax.cond(always, exchange, lambda proj: proj, after(proj, share))
-    with jax.named_scope("solve"):
-        near = solve_call(proj, gram, tri)
-        far = pair_swap(near)
-    with jax.named_scope("update"):
-        out = update_call(core, near, e_near, terms, None)
-        out = update_call(away, far, e_far, terms, out)
-    return out
+            near = all_to_all(copies(proj, devices))
+            near = near.reshape(-1, blocks * width // 128, 128).transpose(1, 0, 2).reshape(-1, 128)
+            return near, pair_swap(near)
+
+    near, far = lax.cond(always, exchange, lambda proj: (proj, proj), after(proj, share))
+    with jax.named_scope("finish"):
+        return finish_call(core, near, far, gram, tri, e_near, e_far, terms)
 
 
 def solution(mesh):

time: 260 us -> 257 us (0.988)
  Pallas kernels: 67.2 us -> 74 us
  local copies, waits for them, and re-layouts: 24.5 us -> 19.1 us
  blocking collectives: 74.9 us -> 72.2 us
    unnamed x26 -> x12, local copies, waits for them, and re-layouts: 24.3 us -> 16.8 us
    pallas_call x3 -> x1, Pallas kernels: 22.1 us -> 28.9 us  [finish_call(): pl.pallas_call(finish_kernel, in_specs=[pl.BlockSpec(memory_space=pltpu.S...]
    all_gather x1, waiting for transfers between devices: 25 us -> 19.7 us  [local(): gram = lax.all_gather(share.reshape(-1, 128), AXES, axis=0, tiled=True)]
    ppermute x3, waiting for transfers between devices: 6.25 us -> 10.4 us  [pair_swap(): lax.ppermute(x, 'col', [(i, i ^ 1) for i in range(lax.axis_size('col'))])]
    all_to_all x2, blocking collectives: 74.9 us -> 72.2 us  [all_to_all(): return lax.all_to_all(x, AXES, 0, 0, tiled=True)]
  transfers between devices with their start and end apart: 6 -> 6, of which waited for: 3 -> 4; matrix products, arithmetic and copies ran while one was open for 3% -> 3% of each run, Pallas kernels for 20% -> 18%
where the time goes in v4:
time: 257 us; the launch traced here: 256 us
  Pallas kernels  74 us (29%)
  blocking collectives  72.2 us (28%)
  waiting for transfers between devices  44.2 us (17%)
  starting transfers between devices  24.3 us (9%)
  local copies, waits for them, and re-layouts  19.1 us (7%)
  between operations  13.5 us (5%)
  other arithmetic  8.81 us (3%)
    all_to_all x2, blocking collectives, all_to_all(): return lax.all_to_all(x, AXES, 0, 0, tiled=True)  72.2 us
    pallas_call x1, Pallas kernels, finish_call(): pl.pallas_call(finish_kernel, in_specs=[pl.BlockSpec(memory_space=pltpu.S...  28.9 us
    pallas_call x1, Pallas kernels, gram_call(): pl.pallas_call(gram_kernel, grid_spec=pltpu.PrefetchScalarGridSpec(num_sc...  27.1 us
    all_to_all x2, starting transfers between devices, all_to_all(): return lax.all_to_all(x, AXES, 0, 0, tiled=True)  21 us
    all_gather x1, waiting for transfers between devices, local(): gram = lax.all_gather(share.reshape(-1, 128), AXES, axis=0, tiled=True)  19.7 us
    pallas_call x2, Pallas kernels, proj_call(): pl.pallas_call(proj_kernel, grid_spec=pltpu.PrefetchScalarGridSpec(num_sc...  18 us
    unnamed x12, local copies, waits for them, and re-layouts  16.8 us
    all_to_all x2, waiting for transfers between devices, all_to_all(): return lax.all_to_all(x, AXES, 0, 0, tiled=True)  14.2 us
  transfers between devices with their start and end apart: 6, of which 4 were waited for; matrix products, arithmetic and copies ran while one was open for 3% of the time, Pallas kernels for 18%

profile of v4, /device:TPU:1, one launch (start us, length us, event | category | flops | bytes accessed | tf_op | source)
XLA Modules:
  0.0 256.1 jit_solution(13041331301872287880)
XLA Ops:
  6.5 11.5 %all-to-all-start.2 = ((f32[128,4,1536]{2,1,0:T(4,128)}), f32[128,4,1536]{2,1,0:T(4,128)S(1)}, u32[]{:S(2)}, u32[]{:S(2)}) async-start(f32[128,4,1536]{2,1,0:T(4,128)} %bitcast.24), calls=%async_computation.2 | async-start | bytes 6291456 | tf_op jit(solution)/shard_map/rows/all_to_all | solution.py:261
  18.0 0.0 copy-start
  18.1 4.6 %copy-done = f32[8,1536,256]{2,1,0:T(8,128)S(1)} copy-done((f32[8,1536,256]{2,1,0:T(8,128)S(1)}, f32[8,1536,256]{2,1,0:T(8,128)}, u32[]{:S(2)}) %copy-start) | copy-done | bytes 12582936
  22.6 27.1 %gram.1 = (f32[128,7,8,128]{3,2,1,0:T(8,128)}, f32[128,7,8,128]{3,2,1,0:T(8,128)}) custom-call(s32[1]{0:T(128)} %bitcast.8.core_ref.half_ref, f32[8,1536,256]{2,1,0:T(8,128)S(1)} %copy-done), custom_call_target="tpu_custom_call" | custom-call | flops 33822867456 | bytes 20000000 | tf_op jit(solution)/shard_map/gram/gram/pallas_call | solution.py:71
  49.7 11.6 %conditional.2 = (f32[7168,128]{1,0:T(8,128)}) conditional(s32[]{:T(128)} %convert_element_type.4, f32[7168,128]{1,0:T(8,128)} %bitcast.18, (f32[128,7,8,128]{3,2,1,0:T(8,128)}, f32[7168,128]{1,0:T(8,128)}) %tuple.33), branch_computations={%region_0.0_spmd, %region_1.0_spmd} | conditional | flops 917504 | bytes 25690160 | solution.py:288
  49.7 1.1 collective-permute-start
  50.8 6.2 %collective-permute-done = f32[7168,128]{1,0:T(8,128)S(1)} collective-permute-done((f32[7168,128]{1,0:T(8,128)}, f32[7168,128]{1,0:T(8,128)S(1)}, u32[]{:S(2)}, u32[]{:S(2)}) %collective-permute-start) | collective-permute-done | bytes 3670048 | tf_op jit(solution)/shard_map/gram/cond/branch_1_fun/ppermute | solution.py:257
  57.0 4.2 %add.4 = f32[7168,128]{1,0:T(8,128)} add(f32[7168,128]{1,0:T(8,128)} %get-tuple-element.16, f32[7168,128]{1,0:T(8,128)S(1)} %collective-permute-done) | non-fusion elementwise | flops 917504 | bytes 11010048 | tf_op jit(solution)/shard_map/gram/cond/branch_1_fun/add | solution.py:288
  61.3 9.5 %all-to-all-start.3 = ((f32[128,56,128]{2,1,0:T(8,128)}), f32[128,56,128]{2,1,0:T(8,128)}, u32[]{:S(2)}, u32[]{:S(2)}) async-start(f32[128,56,128]{2,1,0:T(8,128)} %bitcast.20), calls=%async_computation.3 | async-start | bytes 7340032 | tf_op jit(solution)/shard_map/gram/all_to_all | solution.py:261
  70.8 0.0 all-gather.2.cloned.1.call-start
  70.8 4.6 %copy-done.1 = f32[8,1536,256]{2,1,0:T(8,128)S(1)} copy-done((f32[8,1536,256]{2,1,0:T(8,128)S(1)}, f32[8,1536,256]{2,1,0:T(8,128)}, u32[]{:S(2)}) %copy-start.1) | copy-done | bytes 12582936
  75.4 7.2 %proj.3 = (f32[4096,128]{1,0:T(8,128)S(1)}, f32[1536,256]{1,0:T(8,128)S(1)}) custom-call(s32[1]{0:T(128)S(6)} %sub.3.half_ref, f32[128,4,1536]{2,1,0:T(4,128)S(1)} %all-to-all-done.2.x_ref, f32[8,1536,256]{2,1,0:T(8,128)S(1)} %copy-done.1), custom_call_target="tpu_custom_call" | custom-call | flops 4831838208 | bytes 16000000 | tf_op jit(solution)/shard_map/proj/proj/pallas_call | solution.py:130
  82.6 1.1 copy-done.4
  83.8 1.1 collective-permute-start.2
  84.9 10.8 %proj.2 = (f32[4096,128]{1,0:T(8,128)S(1)}, f32[1536,256]{1,0:T(8,128)S(1)}, bf16[8,1536,256]{2,1,0:T(8,128)(2,1)S(1)}, bf16[8,1536,256]{2,1,0:T(8,128)(2,1)S(1)}) custom-call(s32[1]{0:T(128)} %bitcast.8.core_ref.half_ref, f32[128,4,1536]{2,1,0:T(4,128)S(1)} %all-to-all-done.2.x_ref, f32[8,1536,256]{2,1,0:T(8,128)} %h_ref.5), custom_call_target="tpu_custom_call" | custom-call | flops 4831838208 | bytes 16000000 | tf_op jit(solution)/shard_map/proj/proj/pallas_call | solution.py:130
  95.7 2.7 %copy-done.2 = bf16[8,1536,256]{2,1,0:T(8,128)(2,1)} copy-done((bf16[8,1536,256]{2,1,0:T(8,128)(2,1)}, bf16[8,1536,256]{2,1,0:T(8,128)(2,1)S(1)}, u32[]{:S(2)}) %copy-start.2) | copy-done | bytes 6291480
  98.4 2.6 %copy-done.3 = bf16[8,1536,256]{2,1,0:T(8,128)(2,1)} copy-done((bf16[8,1536,256]{2,1,0:T(8,128)(2,1)}, bf16[8,1536,256]{2,1,0:T(8,128)(2,1)S(1)}, u32[]{:S(2)}) %copy-start.3) | copy-done | bytes 6291480
  101.0 1.2 copy-done.5
  102.2 1.6 add.6
  103.8 14.2 %all-to-all-done.3 = f32[128,56,128]{2,1,0:T(8,128)} async-done(((f32[128,56,128]{2,1,0:T(8,128)}), f32[128,56,128]{2,1,0:T(8,128)}, u32[]{:S(2)}, u32[]{:S(2)}) %all-to-all-start.3) | async-done | bytes 3670048 | tf_op jit(solution)/shard_map/gram/all_to_all | solution.py:261
  118.0 2.9 %reduce_sum.18 = f32[2,56,128]{2,1,0:T(8,128)} reduce(f32[64,2,56,128]{3,2,1,0:T(8,128)} %bitcast.14, f32[]{:T(128)} %constant.15.clone.1), dimensions={0}, to_apply=%region_2.0 | reduce | flops 903168 | bytes 3727364 | tf_op jit(solution)/shard_map/gram/reduce_sum | solution.py:265
  120.8 0.0 all-gather.2.cloned.1.call-update
  120.9 79.8 %conditional.3 = (f32[4096,128]{1,0:T(8,128)}, f32[4096,128]{1,0:T(8,128)}) conditional(s32[]{:T(128)} %convert_element_type.4, f32[4096,128]{1,0:T(8,128)} %add.6, f32[4096,128]{1,0:T(8,128)} %add.6), branch_computations={%region_3.0_spmd, %region_4.0_spmd} | conditional | flops 516096 | bytes 25231420 | solution.py:308
  120.9 35.9 %all_to_all.31 = f32[128,32,128]{2,1,0:T(8,128)S(1)} all-to-all(f32[128,32,128]{2,1,0:T(8,128)} %bitcast.1), channel_id=1, replica_groups=mesh['row'=16,'col'=8] {'row','col'}, dimensions={0} | all-to-all | bytes 4194304 | tf_op jit(solution)/shard_map/cond/branch_1_fun/proj/all_to_all | solution.py:261
  156.8 0.1 reduce_sum.16
  156.9 0.3 broadcast_in_dim.0
  157.2 36.2 %all_to_all.32 = f32[128,32,128]{2,1,0:T(8,128)S(1)} all-to-all(f32[128,32,128]{2,1,0:T(8,128)S(1)} %bitcast.23), channel_id=1, replica_groups=mesh['row'=16,'col'=8] {'row','col'}, dimensions={0} | all-to-all | bytes 4194304 | tf_op jit(solution)/shard_map/cond/branch_1_fun/proj/all_to_all | solution.py:261
  193.4 2.0 copy.4
  195.4 1.1 collective-permute-start.1
  196.5 4.1 %collective-permute-done.1 = f32[4096,128]{1,0:T(8,128)} collective-permute-done((f32[4096,128]{1,0:T(8,128)}, f32[4096,128]{1,0:T(8,128)}, u32[]{:S(2)}, u32[]{:S(2)}) %collective-permute-start.1) | collective-permute-done | bytes 2097184 | tf_op jit(solution)/shard_map/cond/branch_1_fun/proj/ppermute | solution.py:257
  200.6 19.7 %all-gather.2.cloned.1.call-done = f32[14336,128]{1,0:T(8,128)} async-done(((f32[112,128]{1,0:T(8,128)}), f32[14336,128]{1,0:T(8,128)}) %all-gather.2.cloned.1.call-update) | async-done | bytes 7340048 | tf_op jit(solution)/shard_map/gram/all_gather | solution.py:298
  220.3 28.9 %finish.1 = f32[1536,512]{1,0:T(8,128)} custom-call(s32[1]{0:T(128)} %bitcast.8.core_ref.half_ref, f32[4096,128]{1,0:T(8,128)} %get-tuple-element.40.near_ref, f32[4096,128]{1,0:T(8,128)} %get-tuple-element.41.far_ref, f32[128,14,8,128]{3,2,1,0:T(8,128)} %bitcast.26, f32[8,256,256]{2,1,0:T(8,128)} %tri_ref.1, f32[1536,256]{1,0:T(8,128)} %copy-done.5, ...), custom_call_target="tpu_custom_call" | custom-call | flops 16999999488 | bytes 35000000 | tf_op jit(solution)/shard_map/finish/finish/pallas_call | solution.py:227
  (7 shorter events, 0.0 us)
Async XLA Ops:
  6.5 54.7 %all-to-all-start.2 = ((f32[128,4,1536]{2,1,0:T(4,128)}), f32[128,4,1536]{2,1,0:T(4,128)S(1)}, u32[]{:S(2)}, u32[]{:S(2)}) async-start(f32[128,4,1536]{2,1,0:T(4,128)} %bitcast.24), calls=%async_computation.2 | async-start | bytes 6291456 | tf_op jit(solution)/shard_map/rows/all_to_all | solution.py:261
  18.0 4.6 %copy-start = (f32[8,1536,256]{2,1,0:T(8,128)S(1)}, f32[8,1536,256]{2,1,0:T(8,128)}, u32[]{:S(2)}) copy-start(f32[8,1536,256]{2,1,0:T(8,128)} %h_ref.5) | copy-start | bytes 37748740
  49.7 7.3 %collective-permute-start = (f32[7168,128]{1,0:T(8,128)}, f32[7168,128]{1,0:T(8,128)S(1)}, u32[]{:S(2)}, u32[]{:S(2)}) collective-permute-start(f32[7168,128]{1,0:T(8,128)} %bitcast.27), channel_id=1, source_target_pairs={{0,1},{1,0},{2,3},{3,2},{4,5},{5,4},{6,7},{7,6},{8,9},{9,8},{10,11... | collective-permute-start | bytes 11010056 | tf_op jit(solution)/shard_map/gram/cond/branch_1_fun/ppermute | solution.py:257
  61.3 56.7 %all-to-all-start.3 = ((f32[128,56,128]{2,1,0:T(8,128)}), f32[128,56,128]{2,1,0:T(8,128)}, u32[]{:S(2)}, u32[]{:S(2)}) async-start(f32[128,56,128]{2,1,0:T(8,128)} %bitcast.20), calls=%async_computation.3 | async-start | bytes 7340032 | tf_op jit(solution)/shard_map/gram/all_to_all | solution.py:261
  70.8 149.5 %all-gather.2.cloned.1.call-start = ((), (), s32[]{:S(2)}) async-start(), calls=%async_computation.4 | async-start | bytes 7397376 | tf_op jit(solution)/shard_map/gram/all_gather | solution.py:298
  70.8 4.6 %copy-start.1 = (f32[8,1536,256]{2,1,0:T(8,128)S(1)}, f32[8,1536,256]{2,1,0:T(8,128)}, u32[]{:S(2)}) copy-start(f32[8,1536,256]{2,1,0:T(8,128)} %h_ref.5) | copy-start | bytes 37748740
  82.6 1.2 copy-start.4
  83.8 18.5 %collective-permute-start.2 = (f32[4096,128]{1,0:T(8,128)S(1)}, f32[4096,128]{1,0:T(8,128)S(1)}, u32[]{:S(2)}, u32[]{:S(2)}) collective-permute-start(f32[4096,128]{1,0:T(8,128)S(1)} %get-tuple-element.36), channel_id=1, source_target_pairs={{0,1},{1,0},{2,3},{3,2},{4,5},{5,4},{6,7},{7,6},{8,9},{9,8},{10,11... | collective-permute-start | bytes 6291464 | tf_op jit(solution)/shard_map/proj/ppermute | solution.py:257
  95.7 2.7 %copy-start.2 = (bf16[8,1536,256]{2,1,0:T(8,128)(2,1)}, bf16[8,1536,256]{2,1,0:T(8,128)(2,1)S(1)}, u32[]{:S(2)}) copy-start(bf16[8,1536,256]{2,1,0:T(8,128)(2,1)S(1)} %get-tuple-element.44.hh_ref) | copy-start | bytes 18874372
  98.4 2.6 %copy-start.3 = (bf16[8,1536,256]{2,1,0:T(8,128)(2,1)}, bf16[8,1536,256]{2,1,0:T(8,128)(2,1)S(1)}, u32[]{:S(2)}) copy-start(bf16[8,1536,256]{2,1,0:T(8,128)(2,1)S(1)} %get-tuple-element.45.hl_ref) | copy-start | bytes 18874372
  101.0 1.2 copy-start.5
  195.4 5.2 %collective-permute-start.1 = (f32[4096,128]{1,0:T(8,128)}, f32[4096,128]{1,0:T(8,128)}, u32[]{:S(2)}, u32[]{:S(2)}) collective-permute-start(f32[4096,128]{1,0:T(8,128)} %bitcast.6), channel_id=1, source_target_pairs={{0,1},{1,0},{2,3},{3,2},{4,5},{5,4},{6,7},{7,6},{8,9},{9,8},{10,11... | collective-permute-start | bytes 6291464 | tf_op jit(solution)/shard_map/cond/branch_1_fun/proj/ppermute | solution.py:257
Sparse Core Ops, SparseCore 0:
  121.0 99.2 all-gather.1

commit v5 on v4

--- a/solution.py
+++ b/solution.py
@@ -167,8 +167,9 @@
     tris = [pltpu.make_async_copy(tri_ref.at[b], tri.at[b], t_sems.at[b]) for b in range(blocks)]
     parts = [pl.ds(i * chunks, chunks) for i in range(runs)]
     strips = [pltpu.make_async_copy(g_ref.at[parts[i]], g.at[parts[i]], g_sems.at[i]) for i in range(runs)]
-    terms = [pltpu.make_async_copy(hh_ref.at[b], hh.at[b], h_sems.at[b]) for b in range(blocks)]
-    terms += [pltpu.make_async_copy(hl_ref.at[b], hl.at[b], h_sems.at[blocks + b]) for b in range(blocks)]
+    blks = [slice(b * width, (b + 1) * width) for b in range(blocks)]
+    terms = [pltpu.make_async_copy(hh_ref.at[b], hh.at[:, blks[b]], h_sems.at[b]) for b in range(blocks)]
+    terms += [pltpu.make_async_copy(hl_ref.at[b], hl.at[:, blks[b]], h_sems.at[blocks + b]) for b in range(blocks)]
     for copy in small[:2] + tris[:1]:
         copy.start()
     for copy in strips[:1] + tris[1:3] + strips[1:] + tris[3:]:
@@ -189,14 +190,14 @@
                 strips[pair].wait()
             block = [g[parts[pair % runs], half * deep + pair // runs].reshape(width, 128) for half in range(2)]
             high, low = split(jnp.concatenate(block, axis=1))
-            p = p - dot3(ch[a], cl[a], high, low)
+            p = p - dot3(ch[:, blks[a]], cl[:, blks[a]], high, low)
         high, low = split(p)
         tris[b].wait()
         t_high, t_low = split(tri[b])
         coef = dot(high, t_high, NT) + (dot(high, t_low, NT) + dot(low, t_high, NT))
         high, low = split(coef)
-        ch[b] = high
-        cl[b] = low
+        ch[:, blks[b]] = high
+        cl[:, blks[b]] = low
         if b >= 2:
             for copy in later[(b - 2) * 3:(b - 1) * 3]:
                 copy.start()
@@ -209,10 +210,8 @@
         at = slice(r * tile, (r + 1) * tile)
         one, two = e_near[at, :], e_far[at, :]
         total = jnp.concatenate([jnp.where(first_core, one, two), jnp.where(first_core, two, one)], axis=1)
-        for b in range(blocks):
-            high = hh[b, at, :]
-            total = total - (dot(high, ch[b], NT) + (dot(high, cl[b], NT) + dot(hl[b, at, :], ch[b], NT)))
-        out[at, :] = total
+        high = hh[at, :]
+        out[at, :] = total - (dot(high, ch[...], NT) + (dot(high, cl[...], NT) + dot(hl[at, :], ch[...], NT)))
         sent.append(pltpu.make_async_copy(out.at[at, :], out_ref.at[at, :], out_sems.at[r]))
         sent[-1].start()
     for copy in sent:
@@ -236,11 +235,11 @@
             pltpu.VMEM(tri.shape, F32),
             pltpu.VMEM(e_near.shape, F32),
             pltpu.VMEM(e_far.shape, F32),
-            pltpu.VMEM(terms[0].shape, BF),
-            pltpu.VMEM(terms[1].shape, BF),
+            pltpu.VMEM((rows, blocks * width), BF),
+            pltpu.VMEM((rows, blocks * width), BF),
             pltpu.VMEM((rows, 2 * n), F32),
-            pltpu.VMEM((blocks, 2 * n, width), BF),
-            pltpu.VMEM((blocks, 2 * n, width), BF),
+            pltpu.VMEM((2 * n, blocks * width), BF),
+            pltpu.VMEM((2 * n, blocks * width), BF),
             dma((4,)),
             dma((blocks,)),
             dma((8 * gram.shape[0] // width,)),
@@ -257,8 +256,8 @@
     return lax.ppermute(x, "col", [(i, i ^ 1) for i in range(lax.axis_size("col"))])
 
 
-def all_to_all(x):
-    return lax.all_to_all(x, AXES, 0, 0, tiled=True)
+def all_to_all(x, axes=AXES):
+    return lax.all_to_all(x, axes, 0, 0, tiled=True)
 
 
 def sums(got, devices):
@@ -286,7 +285,7 @@
     with jax.named_scope("gram"):
         keep, send = (part.reshape(-1, 128) for part in gram_call(core, house, devices))
         keep = lax.cond(always, lambda keep, send: keep + pair_swap(send), lambda keep, send: keep, keep, send)
-        got = all_to_all(after(keep, x))
+        got = all_to_all(after(keep, x), AXES[::-1])
     with jax.named_scope("proj"):
         send, e_far = proj_call(away, x, house, False)
         send = pair_swap(send)
@@ -294,8 +293,8 @@
         proj = proj + send
     with jax.named_scope("gram"):
         got, proj = lax.optimization_barrier((got, proj))
-        share = sums(got, devices)
-        gram = lax.all_gather(share.reshape(-1, 128), AXES, axis=0, tiled=True)
+        share = jnp.sum(got.reshape(lax.axis_size("col") // 2, 2, lax.axis_size("row"), -1, 128), axis=(0, 2))
+        gram = lax.all_gather(share.reshape(-1, 128), AXES[::-1], axis=0, tiled=True)
         gram = gram.reshape(devices, -1, 8, 128)
 
     def exchange(proj):

time: 257 us -> 255 us (level)
    reduce_sum x2 -> x1, other arithmetic: 3 us -> 0.14 us  [sums(): return jnp.sum(got.reshape(devices // 2, 2, -1, 128), axis=0)]
    reduce_sum x0 -> x1, other arithmetic: none -> 2.85 us  [local(): jnp.sum(got.reshape(lax.axis_size('col') // 2, 2, lax.axis_size('row'), -...]
where the time goes in v5:
time: 255 us; the launch traced here: 254 us
  Pallas kernels  73.6 us (29%)
  blocking collectives  71.6 us (28%)
  waiting for transfers between devices  43.5 us (17%)
  starting transfers between devices  24.3 us (10%)
  local copies, waits for them, and re-layouts  19.1 us (7%)
  between operations  13.5 us (5%)
  other arithmetic  8.81 us (3%)
    all_to_all x2, blocking collectives, all_to_all(): return lax.all_to_all(x, axes, 0, 0, tiled=True)  71.6 us
    pallas_call x1, Pallas kernels, finish_call(): pl.pallas_call(finish_kernel, in_specs=[pl.BlockSpec(memory_space=pltpu.S...  28.5 us
    pallas_call x1, Pallas kernels, gram_call(): pl.pallas_call(gram_kernel, grid_spec=pltpu.PrefetchScalarGridSpec(num_sc...  27.1 us
    all_to_all x2, starting transfers between devices, all_to_all(): return lax.all_to_all(x, axes, 0, 0, tiled=True)  21 us
    all_gather x1, waiting for transfers between devices, local(): lax.all_gather(share.reshape(-1, 128), AXES[::-1], axis=0, tiled=True)  19.4 us
    pallas_call x2, Pallas kernels, proj_call(): pl.pallas_call(proj_kernel, grid_spec=pltpu.PrefetchScalarGridSpec(num_sc...  18 us
    unnamed x12, local copies, waits for them, and re-layouts  16.8 us
    all_to_all x2, waiting for transfers between devices, all_to_all(): return lax.all_to_all(x, axes, 0, 0, tiled=True)  13.7 us
  transfers between devices with their start and end apart: 6, of which 4 were waited for; matrix products, arithmetic and copies ran while one was open for 3% of the time, Pallas kernels for 18%

profile of v5, /device:TPU:1, one launch (start us, length us, event | category | flops | bytes accessed | tf_op | source)
XLA Modules:
  0.0 254.4 jit_solution(12038005546585331876)
XLA Ops:
  6.5 11.5 %all-to-all-start.2 = ((f32[128,4,1536]{2,1,0:T(4,128)}), f32[128,4,1536]{2,1,0:T(4,128)S(1)}, u32[]{:S(2)}, u32[]{:S(2)}) async-start(f32[128,4,1536]{2,1,0:T(4,128)} %bitcast.24), calls=%async_computation.2 | async-start | bytes 6291456 | tf_op jit(solution)/shard_map/rows/all_to_all | solution.py:260
  18.0 0.0 copy-start
  18.1 4.6 %copy-done = f32[8,1536,256]{2,1,0:T(8,128)S(1)} copy-done((f32[8,1536,256]{2,1,0:T(8,128)S(1)}, f32[8,1536,256]{2,1,0:T(8,128)}, u32[]{:S(2)}) %copy-start) | copy-done | bytes 12582936
  22.6 27.1 %gram.1 = (f32[128,7,8,128]{3,2,1,0:T(8,128)}, f32[128,7,8,128]{3,2,1,0:T(8,128)}) custom-call(s32[1]{0:T(128)} %bitcast.8.core_ref.half_ref, f32[8,1536,256]{2,1,0:T(8,128)S(1)} %copy-done), custom_call_target="tpu_custom_call" | custom-call | flops 33822867456 | bytes 20000000 | tf_op jit(solution)/shard_map/gram/gram/pallas_call | solution.py:71
  49.7 11.6 %conditional.2 = (f32[7168,128]{1,0:T(8,128)}) conditional(s32[]{:T(128)} %convert_element_type.4, f32[7168,128]{1,0:T(8,128)} %bitcast.18, (f32[128,7,8,128]{3,2,1,0:T(8,128)}, f32[7168,128]{1,0:T(8,128)}) %tuple.33), branch_computations={%region_0.0_spmd, %region_1.0_spmd} | conditional | flops 917504 | bytes 25690160 | solution.py:287
  49.7 1.1 collective-permute-start
  50.8 6.2 %collective-permute-done = f32[7168,128]{1,0:T(8,128)S(1)} collective-permute-done((f32[7168,128]{1,0:T(8,128)}, f32[7168,128]{1,0:T(8,128)S(1)}, u32[]{:S(2)}, u32[]{:S(2)}) %collective-permute-start) | collective-permute-done | bytes 3670048 | tf_op jit(solution)/shard_map/gram/cond/branch_1_fun/ppermute | solution.py:256
  57.0 4.2 %add.4 = f32[7168,128]{1,0:T(8,128)} add(f32[7168,128]{1,0:T(8,128)} %get-tuple-element.16, f32[7168,128]{1,0:T(8,128)S(1)} %collective-permute-done) | non-fusion elementwise | flops 917504 | bytes 11010048 | tf_op jit(solution)/shard_map/gram/cond/branch_1_fun/add | solution.py:287
  61.3 9.5 %all-to-all-start.3 = ((f32[128,56,128]{2,1,0:T(8,128)}), f32[128,56,128]{2,1,0:T(8,128)}, u32[]{:S(2)}, u32[]{:S(2)}) async-start(f32[128,56,128]{2,1,0:T(8,128)} %bitcast.20), calls=%async_computation.3 | async-start | bytes 7340032 | tf_op jit(solution)/shard_map/gram/all_to_all | solution.py:260
  70.8 0.0 all-gather.2.cloned.1.call-start
  70.8 4.6 %copy-done.1 = f32[8,1536,256]{2,1,0:T(8,128)S(1)} copy-done((f32[8,1536,256]{2,1,0:T(8,128)S(1)}, f32[8,1536,256]{2,1,0:T(8,128)}, u32[]{:S(2)}) %copy-start.1) | copy-done | bytes 12582936
  75.4 7.2 %proj.3 = (f32[4096,128]{1,0:T(8,128)S(1)}, f32[1536,256]{1,0:T(8,128)S(1)}) custom-call(s32[1]{0:T(128)S(6)} %sub.3.half_ref, f32[128,4,1536]{2,1,0:T(4,128)S(1)} %all-to-all-done.2.x_ref, f32[8,1536,256]{2,1,0:T(8,128)S(1)} %copy-done.1), custom_call_target="tpu_custom_call" | custom-call | flops 4831838208 | bytes 16000000 | tf_op jit(solution)/shard_map/proj/proj/pallas_call | solution.py:130
  82.6 1.1 copy-done.4
  83.8 1.1 collective-permute-start.2
  84.9 10.8 %proj.2 = (f32[4096,128]{1,0:T(8,128)S(1)}, f32[1536,256]{1,0:T(8,128)S(1)}, bf16[8,1536,256]{2,1,0:T(8,128)(2,1)S(1)}, bf16[8,1536,256]{2,1,0:T(8,128)(2,1)S(1)}) custom-call(s32[1]{0:T(128)} %bitcast.8.core_ref.half_ref, f32[128,4,1536]{2,1,0:T(4,128)S(1)} %all-to-all-done.2.x_ref, f32[8,1536,256]{2,1,0:T(8,128)} %h_ref.5), custom_call_target="tpu_custom_call" | custom-call | flops 4831838208 | bytes 16000000 | tf_op jit(solution)/shard_map/proj/proj/pallas_call | solution.py:130
  95.7 2.7 %copy-done.2 = bf16[8,1536,256]{2,1,0:T(8,128)(2,1)} copy-done((bf16[8,1536,256]{2,1,0:T(8,128)(2,1)}, bf16[8,1536,256]{2,1,0:T(8,128)(2,1)S(1)}, u32[]{:S(2)}) %copy-start.2) | copy-done | bytes 6291480
  98.4 2.6 %copy-done.3 = bf16[8,1536,256]{2,1,0:T(8,128)(2,1)} copy-done((bf16[8,1536,256]{2,1,0:T(8,128)(2,1)}, bf16[8,1536,256]{2,1,0:T(8,128)(2,1)S(1)}, u32[]{:S(2)}) %copy-start.3) | copy-done | bytes 6291480
  101.0 1.2 copy-done.5
  102.2 1.6 add.6
  103.8 13.7 %all-to-all-done.3 = f32[128,56,128]{2,1,0:T(8,128)} async-done(((f32[128,56,128]{2,1,0:T(8,128)}), f32[128,56,128]{2,1,0:T(8,128)}, u32[]{:S(2)}, u32[]{:S(2)}) %all-to-all-start.3) | async-done | bytes 3670048 | tf_op jit(solution)/shard_map/gram/all_to_all | solution.py:260
  117.5 2.9 %reduce_sum.18 = f32[2,56,128]{2,1,0:T(8,128)} reduce(f32[4,2,16,56,128]{4,3,2,1,0:T(8,128)} %bitcast.14, f32[]{:T(128)} %constant.15.clone.1), dimensions={0,2}, to_apply=%region_2.0 | reduce | flops 903168 | bytes 3727364 | tf_op jit(solution)/shard_map/gram/reduce_sum | solution.py:296
  120.3 0.0 all-gather.2.cloned.1.call-update
  120.4 79.2 %conditional.3 = (f32[4096,128]{1,0:T(8,128)}, f32[4096,128]{1,0:T(8,128)}) conditional(s32[]{:T(128)} %convert_element_type.4, f32[4096,128]{1,0:T(8,128)} %add.6, f32[4096,128]{1,0:T(8,128)} %add.6), branch_computations={%region_3.0_spmd, %region_4.0_spmd} | conditional | flops 516096 | bytes 25231420 | solution.py:307
  120.4 35.4 %all_to_all.31 = f32[128,32,128]{2,1,0:T(8,128)S(1)} all-to-all(f32[128,32,128]{2,1,0:T(8,128)} %bitcast.1), channel_id=1, replica_groups=mesh['row'=16,'col'=8] {'row','col'}, dimensions={0} | all-to-all | bytes 4194304 | tf_op jit(solution)/shard_map/cond/branch_1_fun/proj/all_to_all | solution.py:260
  155.8 0.1 reduce_sum.16
  155.9 0.3 broadcast_in_dim.0
  156.2 36.2 %all_to_all.32 = f32[128,32,128]{2,1,0:T(8,128)S(1)} all-to-all(f32[128,32,128]{2,1,0:T(8,128)S(1)} %bitcast.23), channel_id=1, replica_groups=mesh['row'=16,'col'=8] {'row','col'}, dimensions={0} | all-to-all | bytes 4194304 | tf_op jit(solution)/shard_map/cond/branch_1_fun/proj/all_to_all | solution.py:260
  192.4 2.0 copy.4
  194.4 1.1 collective-permute-start.1
  195.5 4.1 %collective-permute-done.1 = f32[4096,128]{1,0:T(8,128)} collective-permute-done((f32[4096,128]{1,0:T(8,128)}, f32[4096,128]{1,0:T(8,128)}, u32[]{:S(2)}, u32[]{:S(2)}) %collective-permute-start.1) | collective-permute-done | bytes 2097184 | tf_op jit(solution)/shard_map/cond/branch_1_fun/proj/ppermute | solution.py:256
  199.6 19.4 %all-gather.2.cloned.1.call-done = f32[14336,128]{1,0:T(8,128)} async-done(((f32[112,128]{1,0:T(8,128)}), f32[14336,128]{1,0:T(8,128)}) %all-gather.2.cloned.1.call-update) | async-done | bytes 7340048 | tf_op jit(solution)/shard_map/gram/all_gather | solution.py:297
  219.0 28.5 %finish.1 = f32[1536,512]{1,0:T(8,128)} custom-call(s32[1]{0:T(128)} %bitcast.8.core_ref.half_ref, f32[4096,128]{1,0:T(8,128)} %get-tuple-element.40.near_ref, f32[4096,128]{1,0:T(8,128)} %get-tuple-element.41.far_ref, f32[128,14,8,128]{3,2,1,0:T(8,128)} %bitcast.26, f32[8,256,256]{2,1,0:T(8,128)} %tri_ref.1, f32[1536,256]{1,0:T(8,128)} %copy-done.5, ...), custom_call_target="tpu_custom_call" | custom-call | flops 16999999488 | bytes 35000000 | tf_op jit(solution)/shard_map/finish/finish/pallas_call | solution.py:226
  (7 shorter events, 0.0 us)
Async XLA Ops:
  6.5 54.7 %all-to-all-start.2 = ((f32[128,4,1536]{2,1,0:T(4,128)}), f32[128,4,1536]{2,1,0:T(4,128)S(1)}, u32[]{:S(2)}, u32[]{:S(2)}) async-start(f32[128,4,1536]{2,1,0:T(4,128)} %bitcast.24), calls=%async_computation.2 | async-start | bytes 6291456 | tf_op jit(solution)/shard_map/rows/all_to_all | solution.py:260
  18.0 4.6 %copy-start = (f32[8,1536,256]{2,1,0:T(8,128)S(1)}, f32[8,1536,256]{2,1,0:T(8,128)}, u32[]{:S(2)}) copy-start(f32[8,1536,256]{2,1,0:T(8,128)} %h_ref.5) | copy-start | bytes 37748740
  49.7 7.3 %collective-permute-start = (f32[7168,128]{1,0:T(8,128)}, f32[7168,128]{1,0:T(8,128)S(1)}, u32[]{:S(2)}, u32[]{:S(2)}) collective-permute-start(f32[7168,128]{1,0:T(8,128)} %bitcast.27), channel_id=1, source_target_pairs={{0,1},{1,0},{2,3},{3,2},{4,5},{5,4},{6,7},{7,6},{8,9},{9,8},{10,11... | collective-permute-start | bytes 11010056 | tf_op jit(solution)/shard_map/gram/cond/branch_1_fun/ppermute | solution.py:256
  61.3 56.2 %all-to-all-start.3 = ((f32[128,56,128]{2,1,0:T(8,128)}), f32[128,56,128]{2,1,0:T(8,128)}, u32[]{:S(2)}, u32[]{:S(2)}) async-start(f32[128,56,128]{2,1,0:T(8,128)} %bitcast.20), calls=%async_computation.3 | async-start | bytes 7340032 | tf_op jit(solution)/shard_map/gram/all_to_all | solution.py:260
  70.8 148.3 %all-gather.2.cloned.1.call-start = ((), (), s32[]{:S(2)}) async-start(), calls=%async_computation.4 | async-start | bytes 7397376 | tf_op jit(solution)/shard_map/gram/all_gather | solution.py:297
  70.8 4.6 %copy-start.1 = (f32[8,1536,256]{2,1,0:T(8,128)S(1)}, f32[8,1536,256]{2,1,0:T(8,128)}, u32[]{:S(2)}) copy-start(f32[8,1536,256]{2,1,0:T(8,128)} %h_ref.5) | copy-start | bytes 37748740
  82.6 1.2 copy-start.4
  83.8 18.5 %collective-permute-start.2 = (f32[4096,128]{1,0:T(8,128)S(1)}, f32[4096,128]{1,0:T(8,128)S(1)}, u32[]{:S(2)}, u32[]{:S(2)}) collective-permute-start(f32[4096,128]{1,0:T(8,128)S(1)} %get-tuple-element.36), channel_id=1, source_target_pairs={{0,1},{1,0},{2,3},{3,2},{4,5},{5,4},{6,7},{7,6},{8,9},{9,8},{10,11... | collective-permute-start | bytes 6291464 | tf_op jit(solution)/shard_map/proj/ppermute | solution.py:256
  95.7 2.7 %copy-start.2 = (bf16[8,1536,256]{2,1,0:T(8,128)(2,1)}, bf16[8,1536,256]{2,1,0:T(8,128)(2,1)S(1)}, u32[]{:S(2)}) copy-start(bf16[8,1536,256]{2,1,0:T(8,128)(2,1)S(1)} %get-tuple-element.44.hh_ref) | copy-start | bytes 18874372
  98.4 2.6 %copy-start.3 = (bf16[8,1536,256]{2,1,0:T(8,128)(2,1)}, bf16[8,1536,256]{2,1,0:T(8,128)(2,1)S(1)}, u32[]{:S(2)}) copy-start(bf16[8,1536,256]{2,1,0:T(8,128)(2,1)S(1)} %get-tuple-element.45.hl_ref) | copy-start | bytes 18874372
  101.0 1.2 copy-start.5
  194.4 5.2 %collective-permute-start.1 = (f32[4096,128]{1,0:T(8,128)}, f32[4096,128]{1,0:T(8,128)}, u32[]{:S(2)}, u32[]{:S(2)}) collective-permute-start(f32[4096,128]{1,0:T(8,128)} %bitcast.6), channel_id=1, source_target_pairs={{0,1},{1,0},{2,3},{3,2},{4,5},{5,4},{6,7},{7,6},{8,9},{9,8},{10,11... | collective-permute-start | bytes 6291464 | tf_op jit(solution)/shard_map/cond/branch_1_fun/proj/ppermute | solution.py:256
Sparse Core Ops, SparseCore 0:
  120.5 98.5 all-gather.1
